TPU v7x, 256 devices: a whole 4x4x8 slice. The times are simulated.
256 devices in a mesh: rep: 8 (over y, z_hi), row: 32 (over z_lo, x, core).
Axes of the slice: x: 4, y: 4, z: 8 (z_hi: 2, z_lo: 4; z = z_hi * 4 + z_lo), core: 2. Of those that a mesh axis runs over, the one named last changes fastest.
Arguments:
- delta: bfloat16 [8, 512, 53248], P('rep', 'row'), may hold values from -6 to 6
- q_start: bfloat16 [53248, 64], P('row'), may hold values from -0.02734375 to 0.02734375
- first_moment: float32 [512, 53248], P('row', 'rep'), may hold values from -0.12 to 0.12
- second_moment: float32 [512, 53248], P('row', 'rep'), may hold values from 0.01 to 0.2
Outputs:
- update: float32 [512, 53248], P('row', 'rep')
- new_first: float32 [512, 53248], P('row', 'rep')
- new_second: float32 [512, 53248], P('row', 'rep')
- q_new: float32 [53248, 64], P(('rep', 'row'))
All inputs are finite; a program needn't handle non-finite values.
Results may differ from a plain program's by a relative error of at most 0.0029.
Values may be sent and summed in bfloat16 or wider, within the bound.
No kernel may reach another device: no remote copies, remote signals or barrier semaphores. Data moves between devices by JAX's collectives and lax.ppermute only.
A program may use at most 128 MiB of HBM per device.

v0:
```python
import jax
import jax.numpy as jnp
from jax import lax
from jax.sharding import PartitionSpec as P

beta_first = 0.9
beta_second = 0.95
fix_first = 1.0 / (1.0 - 0.9**10)
fix_second = 1.0 / (1.0 - 0.95**10)
epsilon = 1e-08


def body(delta, q_start, first_moment, second_moment):
    own_delta = delta[0]
    row_count = own_delta.shape[0]
    col_count = own_delta.shape[1]
    rep_count = lax.axis_size("rep")
    block_cols = col_count // rep_count
    delta_cols = own_delta
    p_own = jnp.dot(
        delta_cols,
        lax.all_gather(q_start, "row", axis=0, tiled=True),
        preferred_element_type=jnp.float32,
    )
    p_sum = lax.psum(p_own, "rep")
    gram_part = jnp.dot(
        p_sum.T, p_sum, precision=lax.Precision.HIGHEST, preferred_element_type=jnp.float32
    )
    gram_matrix = lax.psum(gram_part, "row")
    chol_lower = jnp.linalg.cholesky(gram_matrix)
    p_orth = jax.scipy.linalg.solve_triangular(chol_lower, p_sum.T, lower=True).T.astype(
        jnp.bfloat16
    )
    p_wide = p_orth.astype(jnp.float32)
    arrived = lax.all_to_all(own_delta, "rep", split_axis=1, concat_axis=0, tiled=True)
    replica_vals = arrived.reshape(rep_count, row_count, block_cols).astype(jnp.float32)
    mean_square = jnp.sum(jnp.square(replica_vals), axis=0) / rep_count
    delta_cols = own_delta
    q_mine = lax.psum_scatter(
        lax.dot_general(
            delta_cols, p_orth, (((0,), (0,)), ((), ())), preferred_element_type=jnp.float32
        ),
        ("rep", "row"),
        scatter_dimension=0,
        tiled=True,
    )
    q_new = q_mine / rep_count
    q_cols = lax.all_gather(q_new, "row", axis=0, tiled=True)
    approx = jnp.dot(
        p_wide, q_cols.T, precision=lax.Precision.HIGHEST, preferred_element_type=jnp.float32
    )
    new_first = beta_first * first_moment + (1.0 - beta_first) * approx
    new_second = beta_second * second_moment + (1.0 - beta_second) * mean_square
    update = new_first * fix_first / (jnp.sqrt(new_second * fix_second) + epsilon)
    return (update, new_first, new_second, q_new)


def solution(mesh):
    in_specs = (P("rep", "row", None), P("row", None), P("row", "rep"), P("row", "rep"))
    out_specs = (P("row", "rep"), P("row", "rep"), P("row", "rep"), P(("rep", "row"), None))
    return jax.shard_map(body, mesh=mesh, in_specs=in_specs, out_specs=out_specs, check_vma=False)
```

profile of v0, /device:TPU:1, one launch (start us, length us, event | category | flops | bytes accessed | tf_op | source)
XLA Modules:
  0.0 1673.6 jit_solution(357656123676832572)
XLA Ops:
  7.2 0.7 all-gather.4.cloned.1.call-update
  8.0 73.6 %all-gather.4.cloned.1.call-done = bf16[53248,64]{0,1:T(8,128)(2,1)} async-done(((bf16[1664,64]{0,1:T(8,128)(2,1)}), bf16[53248,64]{0,1:T(8,128)(2,1)}) %all-gather.4.cloned.1.call-update) | async-done | bytes 6815760 | tf_op jit(solution)/shard_map/all_gather | solution.py:22
  81.6 5.3 fusion.2
  86.9 26.8 %psum.14 = f32[16,64]{1,0:T(8,128)S(1)} all-reduce(f32[16,64]{1,0:T(8,128)S(1)} %fusion.2), channel_id=1, replica_groups=mesh['rep'=8,'row'=32] {'rep'}, use_global_device_ids=true, to_apply=%region_0.0 | all-reduce | flops 1024 | bytes 8192 | tf_op jit(solution)/shard_map/psum | solution.py:25
  113.7 0.2 fusion.7
  113.9 131.1 %psum.15 = f32[64,64]{0,1:T(8,128)S(1)} all-reduce(f32[64,64]{0,1:T(8,128)S(1)} %fusion.7), channel_id=1, replica_groups=mesh['rep'=8,'row'=32] {'row'}, use_global_device_ids=true, to_apply=%region_1.0 | all-reduce | flops 4096 | bytes 32768 | tf_op jit(solution)/shard_map/psum | solution.py:29
  245.1 5.8 cholesky.16
  251.0 0.6 compare_reduce_fusion
  251.6 0.7 fusion.4
  252.3 4.9 custom-call.7
  257.4 6.8 convolution_bitcast_fusion
  264.1 19.2 %copy.21 = f32[53248,64]{1,0:T(8,128)} copy(f32[53248,64]{0,1:T(8,128)} %convolution_bitcast_fusion) | data formatting | bytes 27262976
  283.3 0.5 copy.23
  283.8 1.7 copy.19
  285.5 3.6 all-to-all-start
  289.3 1307.6 %reduce-scatter.4.cloned.1.call-done = f32[208,64]{1,0:T(8,128)} async-done(((f32[53248,64]{1,0:T(8,128)}), f32[208,64]{1,0:T(8,128)}) %reduce-scatter.4.cloned.1.call-update) | async-done | bytes 53264
  1596.9 1.0 copy.22
  1597.9 0.6 fusion.15
  1598.6 0.3 multiply_reduce_fusion
  1598.9 0.6 broadcast_multiply_fusion
  1599.6 58.6 %all-gather.6.cloned.1.call-done = f32[32,208,64]{1,2,0:T(8,128)} async-done(((f32[1,208,64]{1,2,0:T(8,128)}), f32[32,208,64]{1,2,0:T(8,128)}) %all-gather.6.cloned.1.call-update) | async-done | bytes 1703952 | tf_op jit(solution)/shard_map/all_gather | solution.py:48
  1658.2 2.8 copy.18
  1661.0 2.7 reshape.25
  1663.7 3.4 add_divide_fusion
  (16 shorter events, 0.6 us)
Async XLA Ops:
  7.2 74.4 %all-gather.4.cloned.1.call-start = ((), (), s32[]{:S(2)}) async-start(), calls=%async_computation.2 | async-start | bytes 7028736 | tf_op jit(solution)/shard_map/all_gather | solution.py:22
  7.9 249.5 %copy-start = (bf16[1,16,53248]{2,1,0:T(8,128)(2,1)S(1)}, bf16[1,16,53248]{2,1,0:T(8,128)(2,1)}, u32[]{:S(2)}) copy-start(bf16[1,16,53248]{2,1,0:T(8,128)(2,1)} %param.4) | copy-start | bytes 5111812
  7.9 1589.0 %reduce-scatter.4.cloned.1.call-start = ((), (), s32[]{:S(2)}) async-start(), calls=%async_computation.4 | async-start | bytes 27369472
  285.5 1313.1 %all-to-all-start = ((bf16[16,8,6656]{2,0,1:T(8,128)(2,1)}), bf16[16,8,6656]{2,0,1:T(8,128)(2,1)S(1)}, u32[]{:S(2)}, u32[]{:S(2)}) async-start(bf16[16,8,6656]{2,0,1:T(8,128)(2,1)} %copy.19), calls=%async_computation | async-start | bytes 3407872 | tf_op jit(solution)/shard_map/all_to_all | solution.py:35
  289.1 1369.1 %all-gather.6.cloned.1.call-start = ((), (), s32[]{:S(2)}) async-start(), calls=%async_computation.3 | async-start | bytes 2162688 | tf_op jit(solution)/shard_map/all_gather | solution.py:48
  1661.0 2.7 copy-start.1
  1661.0 2.7 copy-start.2
Sparse Core Ops, SparseCore 0:
  9.8 71.7 all-gather.3
  283.4 1313.4 reduce-scatter.3
  1599.5 58.5 all-gather.5
where the time goes:
time: 1670 us
  waiting for transfers between devices  1440 us (86%)
  blocking collectives  158 us (9%)
  local copies, waits for them, and re-layouts  27.9 us (2%)
    unnamed x4, waiting for transfers between devices  1310 us
    psum x1, blocking collectives, body(): gram_matrix = lax.psum(gram_part, 'row')  131 us
    all_gather x1, waiting for transfers between devices, body(): lax.all_gather(q_start, 'row', axis=0, tiled=True)  73.6 us
    all_gather x1, waiting for transfers between devices, body(): q_cols = lax.all_gather(q_new, 'row', axis=0, tiled=True)  58.6 us
  transfers between devices with their start and end apart: 4, of which 3 were waited for; matrix products, arithmetic and copies ran while one was open for 0% of the time, Pallas kernels for 0%

commit v1 on v0

v1 whole, which is shorter than its diff:
```python
import jax
import jax.numpy as jnp
from jax import lax
from jax.experimental import pallas as pl
from jax.experimental.pallas import tpu as pltpu
from jax.sharding import Mesh, PartitionSpec as P

beta_first = 0.9
beta_second = 0.95
fix_first = 1.0 / (1.0 - 0.9**10)
fix_second = 1.0 / (1.0 - 0.95**10)
epsilon = 1e-08

NAMES = ("y", "zh", "zl", "x", "c")
SIZES = (4, 2, 4, 4, 2)
REP = ("y", "zh")
ROW = ("zl", "x", "c")
REPS = 8
HIGHEST = lax.Precision.HIGHEST
f32 = jnp.float32
bf16 = jnp.bfloat16


def swap(x, axis, bits):
    return lax.ppermute(x, axis, [(i, i ^ bits) for i in range(lax.axis_size(axis))])


def in_order(blocks, place):
    n = len(blocks)
    bit = 1
    while bit < n:
        set_ = (place & bit) != 0
        blocks = [jnp.where(set_, blocks[k ^ bit], blocks[k]) for k in range(n)]
        bit *= 2
    return blocks


def dot(a, b, contract, precision=None):
    return lax.dot_general(a, b, (contract, ((), ())), precision=precision, preferred_element_type=f32)


def p_kernel(starts, *refs):
    shards, blocks, out = refs[:8], refs[8:12], refs[12]
    rank, span = shards[0].shape
    rows = blocks[0].shape[0]
    total = jnp.zeros((4 * rows, rank), f32)
    for k in range(8):
        at = pl.ds(pl.multiple_of(starts[k], 128), span)
        lhs = jnp.concatenate([b[:, at] for b in blocks], axis=0)
        total = total + dot(lhs, shards[k][...], ((1,), (1,)))
    p = total[:rows] + total[rows : 2 * rows] + total[2 * rows : 3 * rows] + total[3 * rows :]
    out[...] = jnp.concatenate([p, jnp.zeros((rows, 128 - rank), f32)], axis=1)


def p_of(starts, shards, blocks):
    vmem = pl.BlockSpec(memory_space=pltpu.VMEM)
    return pl.pallas_call(
        p_kernel,
        out_shape=jax.ShapeDtypeStruct((blocks[0].shape[0], 128), f32),
        in_specs=[pl.BlockSpec(memory_space=pltpu.SMEM)] + [vmem] * 12,
        out_specs=vmem,
        compiler_params=pltpu.CompilerParams(vmem_limit_bytes=32 * 2**20),
        cost_estimate=pl.CostEstimate(flops=2**27, bytes_accessed=3 * 2**20, transcendentals=0),
        name="p_kernel",
    )(starts, *shards, *blocks)


def mid_kernel(p_ref, came, q_out, approx_out):
    half, rank = came.shape[0] // 2, 64
    span = q_out.shape[1]
    p = p_ref[:, :rank]
    gram = dot(p, p, ((0,), (0,)), HIGHEST)
    row = lax.broadcasted_iota(jnp.int32, (rank, rank), 0)
    col = lax.broadcasted_iota(jnp.int32, (rank, rank), 1)
    a = jnp.concatenate([gram, jnp.where(row == col, 1.0, 0.0).astype(f32)], axis=1)
    below = lax.broadcasted_iota(jnp.int32, (rank, 2 * rank), 0)
    scale = jnp.zeros((rank, 1), f32)
    place = lax.broadcasted_iota(jnp.int32, (rank, 1), 0)
    for j in range(rank):
        pivot = a[j : j + 1, :]
        d = pivot[:, j : j + 1]
        factor = jnp.where(below > j, jnp.broadcast_to(a[:, j : j + 1], (rank, 2 * rank)), 0.0)
        a = a - factor * (pivot * (1.0 / d))
        scale = jnp.where(place == j, d, scale)
    inverse = a[:, rank:] * (1.0 / jnp.sqrt(scale))
    p_orth = dot(p, inverse, ((1,), (1,)), HIGHEST).astype(bf16)
    d_cols = came[:, :span]
    q_t = (dot(p_orth, d_cols[:half], ((0,), (0,))) + dot(p_orth, d_cols[half:], ((0,), (0,)))) / REPS
    q_out[...] = q_t
    approx_out[...] = dot(p_orth.astype(f32), q_t, ((1,), (0,)), HIGHEST).astype(bf16)


def middle(p_sum, came, span):
    vmem = pl.BlockSpec(memory_space=pltpu.VMEM)
    rows = came.shape[0]
    return pl.pallas_call(
        mid_kernel,
        out_shape=(
            jax.ShapeDtypeStruct((64, span), f32),
            jax.ShapeDtypeStruct((rows // 2, span), bf16),
        ),
        in_specs=[vmem, vmem],
        out_specs=(vmem, vmem),
        compiler_params=pltpu.CompilerParams(vmem_limit_bytes=32 * 2**20),
        cost_estimate=pl.CostEstimate(flops=2**33, bytes_accessed=2**20, transcendentals=0),
        name="mid_kernel",
    )(p_sum, came)


def body(delta, q_start, first_moment, second_moment):
    own = delta[0]
    rows, cols = own.shape
    rank = q_start.shape[1]
    wide = cols // 4
    block = cols // REPS
    narrow = block // 32
    y = lax.axis_index("y")
    zh = lax.axis_index("zh")

    x, c = lax.axis_index("x"), lax.axis_index("c")

    def part(k):
        return lax.dynamic_slice(own, (0, (y ^ k) * wide), (rows, wide))

    with jax.named_scope("q_z"):
        q_t = q_start.T
        quarter = rank // 4
        shard = jnp.concatenate(
            [
                lax.ppermute(
                    q_t[quarter * s : quarter * (s + 1)],
                    ("y", "zl"),
                    [(a * 4 + b, b * 4 + (a ^ s)) for a in range(4) for b in range(4)],
                )
                for s in range(4)
            ],
            axis=0,
        )
    with jax.named_scope("delta_y"):
        near = [swap(part(k), "y", k) for k in (1, 3)]
    shard, near = lax.optimization_barrier((shard, near))
    far = part(2)
    with jax.named_scope("q_x"):
        shards = [shard] + [swap(shard, "x", k) for k in (1, 3, 2)]
    with jax.named_scope("delta_y2"):
        far = swap(far, "y", 2)
    shards, far = lax.optimization_barrier((shards, far))
    with jax.named_scope("q_c"):
        shards = shards + [swap(s, "c", 1) for s in shards]
    arrived = [part(0), far] + near
    with jax.named_scope("p_part"):
        starts = jnp.stack([((x ^ k) * 2 + (c ^ i)) * (wide // 8) for i in (0, 1) for k in (0, 1, 3, 2)])
        p_part = p_of(starts, shards, arrived)
    with jax.named_scope("sums"):
        vals = [a.astype(f32) for a in arrived]
        d_part = sum(vals)
        s_part = sum(jnp.square(v) for v in vals)

    with jax.named_scope("d_cols"):
        d_send = d_part.astype(bf16).reshape(rows, 64, narrow).transpose(1, 0, 2)
        came = lax.all_to_all(d_send, ("zh",) + ROW, 0, 0, tiled=True)
    with jax.named_scope("p_y"):
        p_part = p_part + (swap(p_part, "y", 1) + swap(p_part, "y", 3)) + swap(p_part, "y", 2)
    with jax.named_scope("p_zh"):
        p_part = p_part + swap(p_part, "zh", 1)
    with jax.named_scope("p_zl"):
        p_z = jnp.stack(in_order([p_part] + [swap(p_part, "zl", k) for k in (1, 2, 3)], lax.axis_index("zl")))
    with jax.named_scope("squares"):
        at = [(0, half * block) for half in (zh, 1 - zh)]
        s_keep, s_send = [lax.dynamic_slice(s_part, start, (rows, block)) for start in at]
        s_send, p_z = lax.optimization_barrier((s_send.astype(bf16), p_z))
        s_came = swap(s_send, "zh", 1)
    with jax.named_scope("p_xc"):
        p_c = jnp.stack(in_order([p_z, swap(p_z, "c", 1)], c), axis=1)
        p_c, came = lax.optimization_barrier((p_c, came))
        p_xc = [p_c] + [swap(p_c, "x", k) for k in (1, 2, 3)]
        p_sum = jnp.stack(in_order(p_xc, x), axis=1).reshape(32 * rows, 128)
    with jax.named_scope("middle"):
        q_t, approx_cols = middle(p_sum, came.reshape(64 * rows, narrow), narrow)
        q_new = q_t.T
    with jax.named_scope("second"):
        approx_cols, s_came = lax.optimization_barrier((approx_cols, s_came))
        mean_square = (s_keep + s_came.astype(f32)) / REPS
        new_second = beta_second * second_moment + (1.0 - beta_second) * mean_square
    with jax.named_scope("approx"):
        approx = lax.all_to_all(
            approx_cols.reshape(32, rows, narrow), ROW, 0, 0, tiled=True
        )
        approx = approx.transpose(1, 0, 2).reshape(rows, block).astype(f32)

    new_first = beta_first * first_moment + (1.0 - beta_first) * approx
    update = new_first * fix_first / (jnp.sqrt(new_second * fix_second) + epsilon)
    return (update, new_first, new_second, q_new)


def solution(mesh):
    fine = Mesh(mesh.devices.reshape(SIZES), NAMES)
    in_specs = (P(REP, ROW, None), P(ROW, None), P(ROW, REP), P(ROW, REP))
    out_specs = (P(ROW, REP), P(ROW, REP), P(ROW, REP), P(REP + ROW, None))
    return jax.shard_map(body, mesh=fine, in_specs=in_specs, out_specs=out_specs, check_vma=False)
```

time: 1670 us -> 120 us (0.07)
  waiting for transfers between devices: 1440 us -> 34.9 us
  blocking collectives: 158 us -> 0 us
  starting transfers between devices: 3.88 us -> 67 us
  local copies, waits for them, and re-layouts: 27.9 us -> 4.39 us
    unnamed x4 -> x0, waiting for transfers between devices: 1310 us -> none
    psum x2 -> x0, blocking collectives: 158 us -> none  [the longest x1 131 us: body(): gram_matrix = lax.psum(gram_part, 'row')]
    all_gather x2 -> x0, waiting for transfers between devices: 132 us -> none  [the longest x1 73.6 us: body(): lax.all_gather(q_start, 'row', axis=0, tiled=True)]
    ppermute x0 -> x26, starting transfers between devices: none -> 46.5 us  [the longest x22 33 us: swap(): lax.ppermute(x, axis, [(i, i ^ bits) for i in range(lax.axis_size(axis))])]
    unnamed x10 -> x6, local copies, waits for them, and re-layouts: 23.4 us -> 0.01 us
    ppermute x0 -> x26, waiting for transfers between devices: none -> 21.8 us  [the longest x22 20.6 us: swap(): lax.ppermute(x, axis, [(i, i ^ bits) for i in range(lax.axis_size(axis))])]
    all_to_all x1 -> x2, starting transfers between devices: 3.59 us -> 20.5 us  [the longest x1 11.6 us: body(): came = lax.all_to_all(d_send, ('zh',) + ROW, 0, 0, tiled=True)]
  transfers between devices with their start and end apart: 4 -> 28, of which waited for: 3 -> 14; matrix products, arithmetic and copies ran while one was open for 0% -> 3% of each run, Pallas kernels for 0% -> 7%
where the time goes in v1:
time: 120 us; the launch traced here: 119 us
  starting transfers between devices  67 us (56%)
  waiting for transfers between devices  34.9 us (29%)
  Pallas kernels  9.25 us (8%)
  local copies, waits for them, and re-layouts  4.39 us (4%)
  other arithmetic  2.85 us (2%)
    ppermute x22, starting transfers between devices, swap(): lax.ppermute(x, axis, [(i, i ^ bits) for i in range(lax.axis_size(axis))])  33 us
    ppermute x22, waiting for transfers between devices, swap(): lax.ppermute(x, axis, [(i, i ^ bits) for i in range(lax.axis_size(axis))])  20.6 us
    ppermute x4, starting transfers between devices, body(): lax.ppermute(q_t[quarter * s:quarter * (s + 1)], ('y', 'zl'), [(a * 4 + b...  13.4 us
    all_to_all x1, starting transfers between devices, body(): came = lax.all_to_all(d_send, ('zh',) + ROW, 0, 0, tiled=True)  11.6 us
    all_to_all x1, waiting for transfers between devices, body(): lax.all_to_all(approx_cols.reshape(32, rows, narrow), ROW, 0, 0, tiled=True)  11.1 us
    all_to_all x1, starting transfers between devices, body(): lax.all_to_all(approx_cols.reshape(32, rows, narrow), ROW, 0, 0, tiled=True)  8.88 us
    pallas_call x1, Pallas kernels, middle(): pl.pallas_call(mid_kernel, out_shape=(jax.ShapeDtypeStruct((64, span), f3...  8.07 us
  transfers between devices with their start and end apart: 28, of which 14 were waited for; matrix products, arithmetic and copies ran while one was open for 3% of the time, Pallas kernels for 7%

profile of v1, /device:TPU:1, one launch (start us, length us, event | category | flops | bytes accessed | tf_op | source)
XLA Modules:
  0.0 119.2 jit_solution(3258114781360996534)
XLA Ops:
  0.7 1.4 %dynamic-slice_bitcast_fusion = (bf16[16,13312]{1,0:T(8,128)(2,1)S(1)}, bf16[16,13312]{1,0:T(8,128)(2,1)S(1)}, bf16[16,13312]{1,0:T(8,128)(2,1)S(1)}) fusion(bf16[1,16,53248]{2,1,0:T(8,128)(2,1)} %param.4, s32[]{:T(128)S(6)} %select_n.112, s32[]{:T(128)S(6)} %select_n.110, s32[]{:T(128)S(6)} %select_n.111), kind=kLoop, calls=%fused_computation.16 | loop fusion | bytes 2555916 | tf_op jit(solution)/shard_map/dynamic_slice | solution.py:123
  2.1 2.2 %collective-permute-start.4 = (bf16[16,13312]{1,0:T(8,128)(2,1)S(1)}, bf16[16,13312]{1,0:T(8,128)(2,1)S(1)}, u32[]{:S(2)}, u32[]{:S(2)}) collective-permute-start(bf16[16,13312]{1,0:T(8,128)(2,1)S(1)} %get-tuple-element.42), channel_id=1, source_target_pairs={{0,64},{64,0},{128,192},{192,128},{1,65},{65,1},{129,193},{193,129... | collective-permute-start | bytes 1277960 | tf_op jit(solution)/shard_map/delta_y/ppermute | solution.py:25
  4.3 1.9 %collective-permute-start.5 = (bf16[16,13312]{1,0:T(8,128)(2,1)S(1)}, bf16[16,13312]{1,0:T(8,128)(2,1)S(1)}, u32[]{:S(2)}, u32[]{:S(2)}) collective-permute-start(bf16[16,13312]{1,0:T(8,128)(2,1)S(1)} %get-tuple-element.43), channel_id=1, source_target_pairs={{0,192},{64,128},{128,64},{192,0},{1,193},{65,129},{129,65},{193,1... | collective-permute-start | bytes 1277960 | tf_op jit(solution)/shard_map/delta_y/ppermute | solution.py:25
  6.9 3.0 %collective-permute-start.1 = (bf16[16,1664]{1,0:T(8,128)(2,1)S(1)}, bf16[16,1664]{1,0:T(8,128)(2,1)S(1)}, u32[]{:S(2)}, u32[]{:S(2)}) collective-permute-start(bf16[16,1664]{1,0:T(8,128)(2,1)S(1)} %get-tuple-element.51), channel_id=1, source_target_pairs={{0,8},{8,72},{16,136},{24,200},{64,0},{72,64},{80,128},{88,192},{1... | collective-permute-start | bytes 159752 | tf_op jit(solution)/shard_map/q_z/ppermute | solution.py:130
  9.9 4.4 %collective-permute-start.2 = (bf16[16,1664]{1,0:T(8,128)(2,1)S(1)}, bf16[16,1664]{1,0:T(8,128)(2,1)S(1)}, u32[]{:S(2)}, u32[]{:S(2)}) collective-permute-start(bf16[16,1664]{1,0:T(8,128)(2,1)S(1)} %get-tuple-element.50), channel_id=1, source_target_pairs={{0,16},{8,80},{16,144},{24,208},{64,24},{72,88},{80,152},{88,216},... | collective-permute-start | bytes 159752 | tf_op jit(solution)/shard_map/q_z/ppermute | solution.py:130
  14.3 5.4 %collective-permute-start.3 = (bf16[16,1664]{1,0:T(8,128)(2,1)S(1)}, bf16[16,1664]{1,0:T(8,128)(2,1)S(1)}, u32[]{:S(2)}, u32[]{:S(2)}) collective-permute-start(bf16[16,1664]{1,0:T(8,128)(2,1)S(1)} %get-tuple-element.49), channel_id=1, source_target_pairs={{0,24},{8,88},{16,152},{24,216},{64,16},{72,80},{80,144},{88,208},... | collective-permute-start | bytes 159752 | tf_op jit(solution)/shard_map/q_z/ppermute | solution.py:130
  22.2 1.8 %collective-permute-start.7 = (bf16[64,1664]{1,0:T(8,128)(2,1)S(1)}, bf16[64,1664]{1,0:T(8,128)(2,1)S(1)}, u32[]{:S(2)}, u32[]{:S(2)}) collective-permute-start(bf16[64,1664]{1,0:T(8,128)(2,1)S(1)} %pad_maximum_fusion.1.refs_0_), channel_id=1, source_target_pairs={{0,6},{2,4},{4,2},{6,0},{1,7},{3,5},{5,3},{7,1},{8,14},{10,12},{12... | collective-permute-start | bytes 638984 | tf_op jit(solution)/shard_map/q_x/ppermute | solution.py:25
  24.7 4.9 %collective-permute-done.9.refs_9_ = bf16[16,13312]{1,0:T(8,128)(2,1)S(1)} collective-permute-done((bf16[16,13312]{1,0:T(8,128)(2,1)S(1)}, bf16[16,13312]{1,0:T(8,128)(2,1)S(1)}, u32[]{:S(2)}, u32[]{:S(2)}) %collective-permute-start.9) | collective-permute-done | bytes 426016 | tf_op jit(solution)/shard_map/delta_y2/ppermute | solution.py:25
  30.0 1.3 %collective-permute-done.8.refs_3_ = bf16[64,1664]{1,0:T(8,128)(2,1)S(1)} collective-permute-done((bf16[64,1664]{1,0:T(8,128)(2,1)S(1)}, bf16[64,1664]{1,0:T(8,128)(2,1)S(1)}, u32[]{:S(2)}, u32[]{:S(2)}) %collective-permute-start.8) | collective-permute-done | bytes 213024 | tf_op jit(solution)/shard_map/q_x/ppermute | solution.py:25
  31.4 4.4 %collective-permute-start.10 = (bf16[64,1664]{1,0:T(8,128)(2,1)S(1)}, bf16[64,1664]{1,0:T(8,128)(2,1)S(1)}, u32[]{:S(2)}, u32[]{:S(2)}) collective-permute-start(bf16[64,1664]{1,0:T(8,128)(2,1)S(1)} %pad_maximum_fusion.1.refs_0_), channel_id=1, source_target_pairs={{0,1},{1,0},{2,3},{3,2},{4,5},{5,4},{6,7},{7,6},{8,9},{9,8},{10,11... | collective-permute-start | bytes 638984 | tf_op jit(solution)/shard_map/q_c/ppermute | solution.py:25
  39.0 3.6 %collective-permute-start.14 = (f32[16,128]{1,0:T(8,128)S(1)}, f32[16,128]{1,0:T(8,128)S(1)}, u32[]{:S(2)}, u32[]{:S(2)}) collective-permute-start(f32[16,128]{1,0:T(8,128)S(1)} %p_kernel.1), channel_id=1, source_target_pairs={{0,64},{64,0},{128,192},{192,128},{1,65},{65,1},{129,193},{193,129... | collective-permute-start | bytes 24584 | tf_op jit(solution)/shard_map/p_y/ppermute | solution.py:25
  42.6 1.9 %collective-permute-start.16 = (f32[16,128]{1,0:T(8,128)S(1)}, f32[16,128]{1,0:T(8,128)S(1)}, u32[]{:S(2)}, u32[]{:S(2)}) collective-permute-start(f32[16,128]{1,0:T(8,128)S(1)} %p_kernel.1), channel_id=1, source_target_pairs={{0,128},{64,192},{128,0},{192,64},{1,129},{65,193},{129,1},{193,65... | collective-permute-start | bytes 24584 | tf_op jit(solution)/shard_map/p_y/ppermute | solution.py:25
  44.5 1.8 %collective-permute-done.15 = f32[16,128]{1,0:T(8,128)S(1)} collective-permute-done((f32[16,128]{1,0:T(8,128)S(1)}, f32[16,128]{1,0:T(8,128)S(1)}, u32[]{:S(2)}, u32[]{:S(2)}) %collective-permute-start.15) | collective-permute-done | bytes 8224 | tf_op jit(solution)/shard_map/p_y/ppermute | solution.py:25
  46.6 4.1 %collective-permute-start.17 = (f32[16,128]{1,0:T(8,128)S(1)}, f32[16,128]{1,0:T(8,128)S(1)}, u32[]{:S(2)}, u32[]{:S(2)}) collective-permute-start(f32[16,128]{1,0:T(8,128)S(1)} %add_add_fusion), channel_id=1, source_target_pairs={{0,32},{32,0},{1,33},{33,1},{2,34},{34,2},{3,35},{35,3},{4,36},{36... | collective-permute-start | bytes 24584 | tf_op jit(solution)/shard_map/p_zh/ppermute | solution.py:25
  53.3 11.6 %all-to-all-start = ((bf16[64,16,208]{2,1,0:T(8,128)(2,1)}), bf16[64,16,208]{2,1,0:T(8,128)(2,1)S(1)}, u32[]{:S(2)}, u32[]{:S(2)}) async-start(bf16[64,16,208]{2,1,0:T(8,128)(2,1)} %bitcast.46), calls=%async_computation | async-start | bytes 1048576 | tf_op jit(solution)/shard_map/d_cols/all_to_all | solution.py:161
  64.9 3.3 %collective-permute-start.18 = (f32[16,128]{1,0:T(8,128)S(1)}, f32[16,128]{1,0:T(8,128)S(1)}, u32[]{:S(2)}, u32[]{:S(2)}) collective-permute-start(f32[16,128]{1,0:T(8,128)S(1)} %add.106), channel_id=1, source_target_pairs={{0,24},{8,16},{16,8},{24,0},{1,25},{9,17},{17,9},{25,1},{2,26},{10... | collective-permute-start | bytes 24584 | tf_op jit(solution)/shard_map/p_zl/ppermute | solution.py:25
  68.7 8.7 %collective-permute-done.18 = f32[16,128]{1,0:T(8,128)S(1)} collective-permute-done((f32[16,128]{1,0:T(8,128)S(1)}, f32[16,128]{1,0:T(8,128)S(1)}, u32[]{:S(2)}, u32[]{:S(2)}) %collective-permute-start.18) | collective-permute-done | bytes 8224 | tf_op jit(solution)/shard_map/p_zl/ppermute | solution.py:25
  78.4 1.4 %collective-permute-start.21 = (f32[4,16,128]{2,1,0:T(8,128)S(1)}, f32[4,16,128]{2,1,0:T(8,128)S(1)}, u32[]{:S(2)}, u32[]{:S(2)}) collective-permute-start(f32[4,16,128]{2,1,0:T(8,128)S(1)} %pad_maximum_fusion.3), channel_id=1, source_target_pairs={{0,1},{1,0},{2,3},{3,2},{4,5},{5,4},{6,7},{7,6},{8,9},{9,8},{10,11... | collective-permute-start | bytes 98312 | tf_op jit(solution)/shard_map/p_xc/ppermute | solution.py:25
  80.7 1.9 %all-to-all-done = bf16[64,16,208]{2,1,0:T(8,128)(2,1)S(1)} async-done(((bf16[64,16,208]{2,1,0:T(8,128)(2,1)}), bf16[64,16,208]{2,1,0:T(8,128)(2,1)S(1)}, u32[]{:S(2)}, u32[]{:S(2)}) %all-to-all-start) | async-done | bytes 426016 | tf_op jit(solution)/shard_map/d_cols/all_to_all | solution.py:161
  83.8 1.7 %collective-permute-start.23 = (f32[4,2,16,128]{3,2,0,1:T(8,128)S(1)}, f32[4,2,16,128]{3,2,0,1:T(8,128)S(1)}, u32[]{:S(2)}, u32[]{:S(2)}) collective-permute-start(f32[4,2,16,128]{3,2,0,1:T(8,128)S(1)} %pad_maximum_fusion.2), channel_id=1, source_target_pairs={{0,4},{2,6},{4,0},{6,2},{1,5},{3,7},{5,1},{7,3},{8,12},{10,14},{12... | collective-permute-start | bytes 196616 | tf_op jit(solution)/shard_map/p_xc/ppermute | solution.py:25
  85.9 2.3 %collective-permute-start.25 = (bf16[16,6656]{1,0:T(8,128)(2,1)S(1)}, bf16[16,6656]{1,0:T(8,128)(2,1)S(1)}, u32[]{:S(2)}, u32[]{:S(2)}) collective-permute-start(bf16[16,6656]{1,0:T(8,128)(2,1)S(1)} %dynamic-slice_convert_fusion), channel_id=1, source_target_pairs={{0,32},{32,0},{1,33},{33,1},{2,34},{34,2},{3,35},{35,3},{4,36},{36... | collective-permute-start | bytes 638984 | tf_op jit(solution)/shard_map/squares/ppermute | solution.py:25
  89.3 8.1 %mid_kernel.1 = (f32[64,208]{1,0:T(8,128)}, bf16[512,208]{1,0:T(8,128)(2,1)}) custom-call(f32[512,128]{1,0:T(8,128)S(1)} %bitcast.48, bf16[1024,208]{1,0:T(8,128)(2,1)S(1)} %bitcast.47), custom_call_target="tpu_custom_call" | custom-call | flops 8589934592 | bytes 1048576 | tf_op jit(solution)/shard_map/middle/mid_kernel/pallas_call | solution.py:96
  97.3 8.9 %all-to-all-start.1 = ((bf16[32,16,208]{2,1,0:T(8,128)(2,1)}), bf16[32,16,208]{2,1,0:T(8,128)(2,1)S(1)}, u32[]{:S(2)}, u32[]{:S(2)}) async-start(bf16[32,16,208]{2,1,0:T(8,128)(2,1)} %bitcast.26), calls=%async_computation.1 | async-start | bytes 524288 | tf_op jit(solution)/shard_map/approx/all_to_all | solution.py:186
  106.2 11.1 %all-to-all-done.1 = bf16[32,16,208]{2,1,0:T(8,128)(2,1)S(1)} async-done(((bf16[32,16,208]{2,1,0:T(8,128)(2,1)}), bf16[32,16,208]{2,1,0:T(8,128)(2,1)S(1)}, u32[]{:S(2)}, u32[]{:S(2)}) %all-to-all-start.1) | async-done | bytes 213024 | tf_op jit(solution)/shard_map/approx/all_to_all | solution.py:186
  (62 shorter events, 17.1 us)
Async XLA Ops:
  2.1 18.8 %collective-permute-start.4 = (bf16[16,13312]{1,0:T(8,128)(2,1)S(1)}, bf16[16,13312]{1,0:T(8,128)(2,1)S(1)}, u32[]{:S(2)}, u32[]{:S(2)}) collective-permute-start(bf16[16,13312]{1,0:T(8,128)(2,1)S(1)} %get-tuple-element.42), channel_id=1, source_target_pairs={{0,64},{64,0},{128,192},{192,128},{1,65},{65,1},{129,193},{193,129... | collective-permute-start | bytes 1277960 | tf_op jit(solution)/shard_map/delta_y/ppermute | solution.py:25
  4.3 16.6 %collective-permute-start.5 = (bf16[16,13312]{1,0:T(8,128)(2,1)S(1)}, bf16[16,13312]{1,0:T(8,128)(2,1)S(1)}, u32[]{:S(2)}, u32[]{:S(2)}) collective-permute-start(bf16[16,13312]{1,0:T(8,128)(2,1)S(1)} %get-tuple-element.43), channel_id=1, source_target_pairs={{0,192},{64,128},{128,64},{192,0},{1,193},{65,129},{129,65},{193,1... | collective-permute-start | bytes 1277960 | tf_op jit(solution)/shard_map/delta_y/ppermute | solution.py:25
  6.2 8.1 %collective-permute-start = (bf16[16,1664]{1,0:T(8,128)(2,1)S(1)}, bf16[16,1664]{1,0:T(8,128)(2,1)S(1)}, u32[]{:S(2)}, u32[]{:S(2)}) collective-permute-start(bf16[16,1664]{1,0:T(8,128)(2,1)S(1)} %get-tuple-element.48), channel_id=1, source_target_pairs={{0,0},{8,64},{16,128},{24,192},{64,8},{72,72},{80,136},{88,200},{1... | collective-permute-start | bytes 159752 | tf_op jit(solution)/shard_map/q_z/ppermute | solution.py:130
  6.9 12.8 %collective-permute-start.1 = (bf16[16,1664]{1,0:T(8,128)(2,1)S(1)}, bf16[16,1664]{1,0:T(8,128)(2,1)S(1)}, u32[]{:S(2)}, u32[]{:S(2)}) collective-permute-start(bf16[16,1664]{1,0:T(8,128)(2,1)S(1)} %get-tuple-element.51), channel_id=1, source_target_pairs={{0,8},{8,72},{16,136},{24,200},{64,0},{72,64},{80,128},{88,192},{1... | collective-permute-start | bytes 159752 | tf_op jit(solution)/shard_map/q_z/ppermute | solution.py:130
  9.9 9.8 %collective-permute-start.2 = (bf16[16,1664]{1,0:T(8,128)(2,1)S(1)}, bf16[16,1664]{1,0:T(8,128)(2,1)S(1)}, u32[]{:S(2)}, u32[]{:S(2)}) collective-permute-start(bf16[16,1664]{1,0:T(8,128)(2,1)S(1)} %get-tuple-element.50), channel_id=1, source_target_pairs={{0,16},{8,80},{16,144},{24,208},{64,24},{72,88},{80,152},{88,216},... | collective-permute-start | bytes 159752 | tf_op jit(solution)/shard_map/q_z/ppermute | solution.py:130
  14.3 6.6 %collective-permute-start.3 = (bf16[16,1664]{1,0:T(8,128)(2,1)S(1)}, bf16[16,1664]{1,0:T(8,128)(2,1)S(1)}, u32[]{:S(2)}, u32[]{:S(2)}) collective-permute-start(bf16[16,1664]{1,0:T(8,128)(2,1)S(1)} %get-tuple-element.49), channel_id=1, source_target_pairs={{0,24},{8,88},{16,152},{24,216},{64,16},{72,80},{80,144},{88,208},... | collective-permute-start | bytes 159752 | tf_op jit(solution)/shard_map/q_z/ppermute | solution.py:130
  19.7 10.0 %collective-permute-start.9 = (bf16[16,13312]{1,0:T(8,128)(2,1)S(1)}, bf16[16,13312]{1,0:T(8,128)(2,1)S(1)}, u32[]{:S(2)}, u32[]{:S(2)}) collective-permute-start(bf16[16,13312]{1,0:T(8,128)(2,1)S(1)} %get-tuple-element.41), channel_id=1, source_target_pairs={{0,128},{64,192},{128,0},{192,64},{1,129},{65,193},{129,1},{193,65... | collective-permute-start | bytes 1277960 | tf_op jit(solution)/shard_map/delta_y2/ppermute | solution.py:25
  20.9 8.8 %collective-permute-start.6 = (bf16[64,1664]{1,0:T(8,128)(2,1)S(1)}, bf16[64,1664]{1,0:T(8,128)(2,1)S(1)}, u32[]{:S(2)}, u32[]{:S(2)}) collective-permute-start(bf16[64,1664]{1,0:T(8,128)(2,1)S(1)} %pad_maximum_fusion.1.refs_0_), channel_id=1, source_target_pairs={{0,2},{2,0},{4,6},{6,4},{1,3},{3,1},{5,7},{7,5},{8,10},{10,8},{12,... | collective-permute-start | bytes 638984 | tf_op jit(solution)/shard_map/q_x/ppermute | solution.py:25
  22.2 7.8 %collective-permute-start.7 = (bf16[64,1664]{1,0:T(8,128)(2,1)S(1)}, bf16[64,1664]{1,0:T(8,128)(2,1)S(1)}, u32[]{:S(2)}, u32[]{:S(2)}) collective-permute-start(bf16[64,1664]{1,0:T(8,128)(2,1)S(1)} %pad_maximum_fusion.1.refs_0_), channel_id=1, source_target_pairs={{0,6},{2,4},{4,2},{6,0},{1,7},{3,5},{5,3},{7,1},{8,14},{10,12},{12... | collective-permute-start | bytes 638984 | tf_op jit(solution)/shard_map/q_x/ppermute | solution.py:25
  24.0 7.3 %collective-permute-start.8 = (bf16[64,1664]{1,0:T(8,128)(2,1)S(1)}, bf16[64,1664]{1,0:T(8,128)(2,1)S(1)}, u32[]{:S(2)}, u32[]{:S(2)}) collective-permute-start(bf16[64,1664]{1,0:T(8,128)(2,1)S(1)} %pad_maximum_fusion.1.refs_0_), channel_id=1, source_target_pairs={{0,4},{2,6},{4,0},{6,2},{1,5},{3,7},{5,1},{7,3},{8,12},{10,14},{12... | collective-permute-start | bytes 638984 | tf_op jit(solution)/shard_map/q_x/ppermute | solution.py:25
  31.4 6.1 %collective-permute-start.10 = (bf16[64,1664]{1,0:T(8,128)(2,1)S(1)}, bf16[64,1664]{1,0:T(8,128)(2,1)S(1)}, u32[]{:S(2)}, u32[]{:S(2)}) collective-permute-start(bf16[64,1664]{1,0:T(8,128)(2,1)S(1)} %pad_maximum_fusion.1.refs_0_), channel_id=1, source_target_pairs={{0,1},{1,0},{2,3},{3,2},{4,5},{5,4},{6,7},{7,6},{8,9},{9,8},{10,11... | collective-permute-start | bytes 638984 | tf_op jit(solution)/shard_map/q_c/ppermute | solution.py:25
  39.0 5.5 %collective-permute-start.14 = (f32[16,128]{1,0:T(8,128)S(1)}, f32[16,128]{1,0:T(8,128)S(1)}, u32[]{:S(2)}, u32[]{:S(2)}) collective-permute-start(f32[16,128]{1,0:T(8,128)S(1)} %p_kernel.1), channel_id=1, source_target_pairs={{0,64},{64,0},{128,192},{192,128},{1,65},{65,1},{129,193},{193,129... | collective-permute-start | bytes 24584 | tf_op jit(solution)/shard_map/p_y/ppermute | solution.py:25
  42.6 3.7 %collective-permute-start.15 = (f32[16,128]{1,0:T(8,128)S(1)}, f32[16,128]{1,0:T(8,128)S(1)}, u32[]{:S(2)}, u32[]{:S(2)}) collective-permute-start(f32[16,128]{1,0:T(8,128)S(1)} %p_kernel.1), channel_id=1, source_target_pairs={{0,192},{64,128},{128,64},{192,0},{1,193},{65,129},{129,65},{193,1... | collective-permute-start | bytes 24584 | tf_op jit(solution)/shard_map/p_y/ppermute | solution.py:25
  42.6 4.0 %collective-permute-start.16 = (f32[16,128]{1,0:T(8,128)S(1)}, f32[16,128]{1,0:T(8,128)S(1)}, u32[]{:S(2)}, u32[]{:S(2)}) collective-permute-start(f32[16,128]{1,0:T(8,128)S(1)} %p_kernel.1), channel_id=1, source_target_pairs={{0,128},{64,192},{128,0},{192,64},{1,129},{65,193},{129,1},{193,65... | collective-permute-start | bytes 24584 | tf_op jit(solution)/shard_map/p_y/ppermute | solution.py:25
  46.6 18.3 %collective-permute-start.17 = (f32[16,128]{1,0:T(8,128)S(1)}, f32[16,128]{1,0:T(8,128)S(1)}, u32[]{:S(2)}, u32[]{:S(2)}) collective-permute-start(f32[16,128]{1,0:T(8,128)S(1)} %add_add_fusion), channel_id=1, source_target_pairs={{0,32},{32,0},{1,33},{33,1},{2,34},{34,2},{3,35},{35,3},{4,36},{36... | collective-permute-start | bytes 24584 | tf_op jit(solution)/shard_map/p_zh/ppermute | solution.py:25
  53.3 29.4 %all-to-all-start = ((bf16[64,16,208]{2,1,0:T(8,128)(2,1)}), bf16[64,16,208]{2,1,0:T(8,128)(2,1)S(1)}, u32[]{:S(2)}, u32[]{:S(2)}) async-start(bf16[64,16,208]{2,1,0:T(8,128)(2,1)} %bitcast.46), calls=%async_computation | async-start | bytes 1048576 | tf_op jit(solution)/shard_map/d_cols/all_to_all | solution.py:161
  64.9 12.4 %collective-permute-start.18 = (f32[16,128]{1,0:T(8,128)S(1)}, f32[16,128]{1,0:T(8,128)S(1)}, u32[]{:S(2)}, u32[]{:S(2)}) collective-permute-start(f32[16,128]{1,0:T(8,128)S(1)} %add.106), channel_id=1, source_target_pairs={{0,24},{8,16},{16,8},{24,0},{1,25},{9,17},{17,9},{25,1},{2,26},{10... | collective-permute-start | bytes 24584 | tf_op jit(solution)/shard_map/p_zl/ppermute | solution.py:25
  68.2 10.1 %collective-permute-start.19 = (f32[16,128]{1,0:T(8,128)S(1)}, f32[16,128]{1,0:T(8,128)S(1)}, u32[]{:S(2)}, u32[]{:S(2)}) collective-permute-start(f32[16,128]{1,0:T(8,128)S(1)} %add.106), channel_id=1, source_target_pairs={{0,16},{8,24},{16,0},{24,8},{1,17},{9,25},{17,1},{25,9},{2,18},{10... | collective-permute-start | bytes 24584 | tf_op jit(solution)/shard_map/p_zl/ppermute | solution.py:25
  68.2 10.1 %collective-permute-start.20 = (f32[16,128]{1,0:T(8,128)S(1)}, f32[16,128]{1,0:T(8,128)S(1)}, u32[]{:S(2)}, u32[]{:S(2)}) collective-permute-start(f32[16,128]{1,0:T(8,128)S(1)} %add.106), channel_id=1, source_target_pairs={{0,8},{8,0},{16,24},{24,16},{1,9},{9,1},{17,25},{25,17},{2,10},{10... | collective-permute-start | bytes 24584 | tf_op jit(solution)/shard_map/p_zl/ppermute | solution.py:25
  82.7 5.5 %collective-permute-start.22 = (f32[4,2,16,128]{3,2,0,1:T(8,128)S(1)}, f32[4,2,16,128]{3,2,0,1:T(8,128)S(1)}, u32[]{:S(2)}, u32[]{:S(2)}) collective-permute-start(f32[4,2,16,128]{3,2,0,1:T(8,128)S(1)} %pad_maximum_fusion.2), channel_id=1, source_target_pairs={{0,6},{2,4},{4,2},{6,0},{1,7},{3,5},{5,3},{7,1},{8,14},{10,12},{12... | collective-permute-start | bytes 196616 | tf_op jit(solution)/shard_map/p_xc/ppermute | solution.py:25
  83.8 4.7 %collective-permute-start.23 = (f32[4,2,16,128]{3,2,0,1:T(8,128)S(1)}, f32[4,2,16,128]{3,2,0,1:T(8,128)S(1)}, u32[]{:S(2)}, u32[]{:S(2)}) collective-permute-start(f32[4,2,16,128]{3,2,0,1:T(8,128)S(1)} %pad_maximum_fusion.2), channel_id=1, source_target_pairs={{0,4},{2,6},{4,0},{6,2},{1,5},{3,7},{5,1},{7,3},{8,12},{10,14},{12... | collective-permute-start | bytes 196616 | tf_op jit(solution)/shard_map/p_xc/ppermute | solution.py:25
  85.5 3.6 %collective-permute-start.24 = (f32[4,2,16,128]{3,2,0,1:T(8,128)S(1)}, f32[4,2,16,128]{3,2,0,1:T(8,128)S(1)}, u32[]{:S(2)}, u32[]{:S(2)}) collective-permute-start(f32[4,2,16,128]{3,2,0,1:T(8,128)S(1)} %pad_maximum_fusion.2), channel_id=1, source_target_pairs={{0,2},{2,0},{4,6},{6,4},{1,3},{3,1},{5,7},{7,5},{8,10},{10,8},{12,... | collective-permute-start | bytes 196616 | tf_op jit(solution)/shard_map/p_xc/ppermute | solution.py:25
  85.9 11.4 %collective-permute-start.25 = (bf16[16,6656]{1,0:T(8,128)(2,1)S(1)}, bf16[16,6656]{1,0:T(8,128)(2,1)S(1)}, u32[]{:S(2)}, u32[]{:S(2)}) collective-permute-start(bf16[16,6656]{1,0:T(8,128)(2,1)S(1)} %dynamic-slice_convert_fusion), channel_id=1, source_target_pairs={{0,32},{32,0},{1,33},{33,1},{2,34},{34,2},{3,35},{35,3},{4,36},{36... | collective-permute-start | bytes 638984 | tf_op jit(solution)/shard_map/squares/ppermute | solution.py:25
  97.3 20.0 %all-to-all-start.1 = ((bf16[32,16,208]{2,1,0:T(8,128)(2,1)}), bf16[32,16,208]{2,1,0:T(8,128)(2,1)S(1)}, u32[]{:S(2)}, u32[]{:S(2)}) async-start(bf16[32,16,208]{2,1,0:T(8,128)(2,1)} %bitcast.26), calls=%async_computation.1 | async-start | bytes 524288 | tf_op jit(solution)/shard_map/approx/all_to_all | solution.py:186
  (7 other events, 54.3 us)

commit v2 on v1

v2 whole, which is shorter than its diff:
```python
import jax
import jax.numpy as jnp
from jax import lax
from jax.experimental import pallas as pl
from jax.experimental.pallas import tpu as pltpu
from jax.sharding import Mesh, PartitionSpec as P

beta_first = 0.9
beta_second = 0.95
fix_first = 1.0 / (1.0 - 0.9**10)
fix_second = 1.0 / (1.0 - 0.95**10)
epsilon = 1e-08

NAMES = ("y", "zh", "zl", "x", "c")
SIZES = (4, 2, 4, 4, 2)
REP = ("y", "zh")
ROW = ("zl", "x", "c")
REPS = 8
HIGHEST = lax.Precision.HIGHEST
f32 = jnp.float32
bf16 = jnp.bfloat16


def swap(x, axis, bits):
    return lax.ppermute(x, axis, [(i, i ^ bits) for i in range(lax.axis_size(axis))])


def in_order(blocks, place):
    n = len(blocks)
    bit = 1
    while bit < n:
        set_ = (place & bit) != 0
        blocks = [jnp.where(set_, blocks[k ^ bit], blocks[k]) for k in range(n)]
        bit *= 2
    return blocks


def dot(a, b, contract, precision=None):
    return lax.dot_general(a, b, (contract, ((), ())), precision=precision, preferred_element_type=f32)


def split_kernel(zh, own, give, keep):
    block = give.shape[2]
    mine, other = pl.multiple_of(zh[0] * block, 128), pl.multiple_of((1 - zh[0]) * block, 128)
    for k in range(4):
        give[k] = own[:, pl.ds(2 * k * block + other, block)]
        keep[k] = own[:, pl.ds(2 * k * block + mine, block)]


def split(zh, own):
    vmem = pl.BlockSpec(memory_space=pltpu.VMEM)
    half = jax.ShapeDtypeStruct((4, own.shape[0], own.shape[1] // 8), own.dtype)
    return pl.pallas_call(
        split_kernel,
        out_shape=(half, half),
        in_specs=[pl.BlockSpec(memory_space=pltpu.SMEM), vmem],
        out_specs=(vmem, vmem),
        compiler_params=pltpu.CompilerParams(vmem_limit_bytes=32 * 2**20),
        cost_estimate=pl.CostEstimate(flops=0, bytes_accessed=2**22, transcendentals=0),
        name="split_kernel",
    )(zh.reshape(1), own)


def p_kernel(places, *refs):
    shards, first, second, out = refs[:8], refs[8], refs[9], refs[10]
    rank, span = shards[0].shape
    rows = first.shape[1]
    total = jnp.zeros((4 * rows, rank), f32)
    for k in range(8):
        at = pl.ds(pl.multiple_of(places[1, k], 128), span)
        late = places[0, k] != 0
        lhs = jnp.where(late, second[:, :, at], first[:, :, at]).reshape(4 * rows, span)
        total = total + dot(lhs, shards[k][...], ((1,), (1,)))
    p = total[:rows] + total[rows : 2 * rows] + total[2 * rows : 3 * rows] + total[3 * rows :]
    out[...] = jnp.concatenate([p, jnp.zeros((rows, 128 - rank), f32)], axis=1)


def p_of(places, shards, first, second):
    vmem = pl.BlockSpec(memory_space=pltpu.VMEM)
    return pl.pallas_call(
        p_kernel,
        out_shape=jax.ShapeDtypeStruct((first.shape[1], 128), f32),
        in_specs=[pl.BlockSpec(memory_space=pltpu.SMEM)] + [vmem] * 10,
        out_specs=vmem,
        compiler_params=pltpu.CompilerParams(vmem_limit_bytes=32 * 2**20),
        cost_estimate=pl.CostEstimate(flops=2**27, bytes_accessed=3 * 2**20, transcendentals=0),
        name="p_kernel",
    )(places, *shards, first, second)


def inverse_factor(gram):
    n = gram.shape[0]
    row = lax.broadcasted_iota(jnp.int32, (n, 2 * n), 0)
    col = lax.broadcasted_iota(jnp.int32, (n, 2 * n), 1)
    a = jnp.concatenate([gram, gram], axis=1)
    a = jnp.where(col < n, a, jnp.where(col == row + n, 1.0, 0.0))
    rows = lax.broadcasted_iota(jnp.int32, (n, 1), 0)
    scale = jnp.zeros((n, 1), f32)
    for j in range(0, n, 4):
        r = [a[j + i : j + i + 1, :] for i in range(4)]
        c = [jnp.broadcast_to(a[:, j + i : j + i + 1], (n, 2 * n)) for i in range(4)]
        g = [[jnp.broadcast_to(r[i][:, j + k : j + k + 1], (1, 2 * n)) for k in range(4)] for i in range(4)]
        for i in range(4):
            inv = 1.0 / g[i][i]
            scale = jnp.where(rows == j + i, g[i][i][:, :1], scale)
            rs = r[i] * inv
            for k in range(i + 1, 4):
                f = g[i][k] * inv
                r[k] = r[k] - f * r[i]
                c[k] = c[k] - f * c[i]
                for l in range(k, 4):
                    g[k][l] = g[k][l] - f * g[i][l]
            a = a - jnp.where(row > j + i, c[i], 0.0) * rs
    return a[:, n:] * (1.0 / jnp.sqrt(scale))


def mid_kernel(p_ref, came, q_out, approx_out):
    half, rank = came.shape[0], 64
    pairs = p_ref[...].reshape(16, half // 32, 2 * rank)
    p = jnp.concatenate([pairs[:, :, :rank], pairs[:, :, rank:]], axis=1).reshape(half, rank)
    inverse = inverse_factor(dot(p, p, ((0,), (0,)), HIGHEST))
    p_orth = dot(p, inverse, ((1,), (1,)), HIGHEST).astype(bf16)
    q_t = dot(p_orth, came[...], ((0,), (0,))) / REPS
    q_out[...] = q_t
    approx_out[...] = dot(p_orth.astype(f32), q_t, ((1,), (0,)), HIGHEST).astype(bf16)


def middle(p_sum, came, span):
    vmem = pl.BlockSpec(memory_space=pltpu.VMEM)
    rows = came.shape[0]
    return pl.pallas_call(
        mid_kernel,
        out_shape=(
            jax.ShapeDtypeStruct((64, span), f32),
            jax.ShapeDtypeStruct((rows, span), bf16),
        ),
        in_specs=[vmem, vmem],
        out_specs=(vmem, vmem),
        compiler_params=pltpu.CompilerParams(vmem_limit_bytes=32 * 2**20),
        cost_estimate=pl.CostEstimate(flops=2**33, bytes_accessed=2**20, transcendentals=0),
        name="mid_kernel",
    )(p_sum, came)


def body(delta, q_start, first_moment, second_moment):
    own = delta[0]
    rows, cols = own.shape
    rank = q_start.shape[1]
    wide = cols // 4
    block = cols // REPS
    narrow = block // 32
    y = lax.axis_index("y")
    zh = lax.axis_index("zh")

    x, c = lax.axis_index("x"), lax.axis_index("c")

    def along_y(a):
        return lax.all_to_all(a, "y", 0, 0, tiled=True)

    give, keep = split(zh, own)

    with jax.named_scope("q_z"):
        q_t = q_start.T
        quarter = rank // 4
        shard = jnp.concatenate(
            [
                lax.ppermute(
                    q_t[quarter * s : quarter * (s + 1)],
                    ("y", "zl"),
                    [(a * 4 + b, b * 4 + (a ^ s)) for a in range(4) for b in range(4)],
                )
                for s in range(4)
            ],
            axis=0,
        )
    with jax.named_scope("delta_give"):
        give = along_y(give)
    shard, give, keep = lax.optimization_barrier((shard, give, keep))
    with jax.named_scope("q_x"):
        shards = [shard] + [swap(shard, "x", k) for k in (1, 3, 2)]
    with jax.named_scope("delta_keep"):
        keep = along_y(keep)
    with jax.named_scope("sums_give"):
        vals = give.astype(f32)
        sums = jnp.stack([jnp.sum(vals, axis=0), jnp.sum(jnp.square(vals), axis=0)]).astype(bf16)
    with jax.named_scope("sums_zh"):
        d_came, s_came = swap(sums, "zh", 1)
    shards, keep = lax.optimization_barrier((shards, keep))
    with jax.named_scope("q_c"):
        shards = shards + [swap(s, "c", 1) for s in shards]
    with jax.named_scope("p_part"):
        at = [((x ^ k) * 2 + (c ^ i)) * (wide // 8) for i in (0, 1) for k in (0, 1, 3, 2)]
        late = [jnp.where(a >= block, 1, 0) == zh for a in at]
        places = jnp.stack([jnp.stack(late).astype(jnp.int32), jnp.stack(at) % block])
        p_part = p_of(places, shards, give, keep)
    with jax.named_scope("sums_keep"):
        vals = keep.astype(f32)
        d_keep = jnp.sum(vals, axis=0)
        s_keep = jnp.sum(jnp.square(vals), axis=0)

    with jax.named_scope("p_y"):
        p_part = p_part + (swap(p_part, "y", 1) + swap(p_part, "y", 3)) + swap(p_part, "y", 2)
    with jax.named_scope("p_zh"):
        p_part = p_part + swap(p_part, "zh", 1)
        p_part, d_came = lax.optimization_barrier((p_part, d_came))
    with jax.named_scope("d_cols"):
        d_rows = (d_keep + d_came.astype(f32)).astype(bf16)
        d_rows = d_rows.reshape(rows, 32, narrow).transpose(1, 0, 2)
        came = lax.all_to_all(d_rows, ROW, 0, 0, tiled=True)
    with jax.named_scope("p_xc"):
        other = swap(p_part, "c", 1)
        pair = jnp.where(c == 0, p_part[:, :rank], other[:, :rank]), jnp.where(c == 0, other[:, :rank], p_part[:, :rank])
        pair = jnp.concatenate(pair, axis=1)
        p_x = jnp.stack(in_order([pair] + [swap(pair, "x", k) for k in (1, 2, 3)], x))
    with jax.named_scope("p_zl"):
        p_x, came = lax.optimization_barrier((p_x, came))
        p_z = [p_x] + [swap(p_x, "zl", k) for k in (1, 2, 3)]
        p_sum = jnp.stack(in_order(p_z, lax.axis_index("zl"))).reshape(16 * rows, 2 * rank)
    with jax.named_scope("second"):
        mean_square = (s_keep + s_came.astype(f32)) / REPS
        new_second = beta_second * second_moment + (1.0 - beta_second) * mean_square
        below = jnp.sqrt(new_second * fix_second) + epsilon
        came, new_second, below = lax.optimization_barrier((came, new_second, below))
    with jax.named_scope("middle"):
        q_t, approx_cols = middle(p_sum, came.reshape(32 * rows, narrow), narrow)
        q_new = q_t.T
    with jax.named_scope("approx"):
        approx = lax.all_to_all(
            approx_cols.reshape(32, rows, narrow), ROW, 0, 0, tiled=True
        )
        approx = approx.transpose(1, 0, 2).reshape(rows, block).astype(f32)

    new_first = beta_first * first_moment + (1.0 - beta_first) * approx
    update = new_first * fix_first / below
    return (update, new_first, new_second, q_new)


def solution(mesh):
    fine = Mesh(mesh.devices.reshape(SIZES), NAMES)
    in_specs = (P(REP, ROW, None), P(ROW, None), P(ROW, REP), P(ROW, REP))
    out_specs = (P(ROW, REP), P(ROW, REP), P(ROW, REP), P(REP + ROW, None))
    return jax.shard_map(body, mesh=fine, in_specs=in_specs, out_specs=out_specs, check_vma=False)
```

time: 120 us -> 115 us (0.958)
  waiting for transfers between devices: 34.9 us -> 17 us
  blocking collectives: 0 us -> 15.5 us
  Pallas kernels: 9.25 us -> 6.92 us
  starting transfers between devices: 67 us -> 65.3 us
  other arithmetic: 2.85 us -> 4.55 us
    all_to_all x0 -> x1, blocking collectives: none -> 15.5 us  [body(): lax.all_to_all(approx_cols.reshape(32, rows, narrow), ROW, 0, 0, tiled=True)]
    ppermute x22 -> x19, waiting for transfers between devices: 20.6 us -> 8.85 us  [swap(): lax.ppermute(x, axis, [(i, i ^ bits) for i in range(lax.axis_size(axis))])]
    all_to_all x2 -> x3, waiting for transfers between devices: 13 us -> 5.15 us  [the longest x1 4.01 us: body(): came = lax.all_to_all(d_rows, ROW, 0, 0, tiled=True)]
    pallas_call x1, Pallas kernels: 8.07 us -> 4.38 us  [middle(): pl.pallas_call(mid_kernel, out_shape=(jax.ShapeDtypeStruct((64, span), f3...]
    all_to_all x2 -> x3, starting transfers between devices: 20.5 us -> 17.1 us  [the longest x2 9.62 us: along_y(): return lax.all_to_all(a, 'y', 0, 0, tiled=True)]
    ppermute x22 -> x19, starting transfers between devices: 33 us -> 36.2 us  [swap(): lax.ppermute(x, axis, [(i, i ^ bits) for i in range(lax.axis_size(axis))])]
    ppermute x4, waiting for transfers between devices: 1.21 us -> 3.03 us  [body(): lax.ppermute(q_t[quarter * s:quarter * (s + 1)], ('y', 'zl'), [(a * 4 + b...]
    add x1, other arithmetic: 0.31 us -> 1.88 us  [body(): below = jnp.sqrt(new_second * fix_second) + epsilon]
  transfers between devices with their start and end apart: 28 -> 26, of which waited for: 14 -> 14; matrix products, arithmetic and copies ran while one was open for 3% -> 5% of each run, Pallas kernels for 7% -> 1%
where the time goes in v2:
time: 115 us
  starting transfers between devices  65.3 us (57%)
  waiting for transfers between devices  17 us (15%)
  blocking collectives  15.5 us (13%)
  Pallas kernels  6.92 us (6%)
  local copies, waits for them, and re-layouts  4.63 us (4%)
  other arithmetic  4.55 us (4%)
    ppermute x19, starting transfers between devices, swap(): lax.ppermute(x, axis, [(i, i ^ bits) for i in range(lax.axis_size(axis))])  36.2 us
    all_to_all x1, blocking collectives, body(): lax.all_to_all(approx_cols.reshape(32, rows, narrow), ROW, 0, 0, tiled=True)  15.5 us
    ppermute x4, starting transfers between devices, body(): lax.ppermute(q_t[quarter * s:quarter * (s + 1)], ('y', 'zl'), [(a * 4 + b...  12 us
    all_to_all x2, starting transfers between devices, along_y(): return lax.all_to_all(a, 'y', 0, 0, tiled=True)  9.62 us
    ppermute x19, waiting for transfers between devices, swap(): lax.ppermute(x, axis, [(i, i ^ bits) for i in range(lax.axis_size(axis))])  8.85 us
    all_to_all x1, starting transfers between devices, body(): came = lax.all_to_all(d_rows, ROW, 0, 0, tiled=True)  7.51 us
    pallas_call x1, Pallas kernels, middle(): pl.pallas_call(mid_kernel, out_shape=(jax.ShapeDtypeStruct((64, span), f3...  4.38 us
    all_to_all x1, waiting for transfers between devices, body(): came = lax.all_to_all(d_rows, ROW, 0, 0, tiled=True)  4.01 us
  transfers between devices with their start and end apart: 26, of which 14 were waited for; matrix products, arithmetic and copies ran while one was open for 5% of the time, Pallas kernels for 1%

profile of v2, /device:TPU:1, one launch (start us, length us, event | category | flops | bytes accessed | tf_op | source)
XLA Modules:
  0.0 114.9 jit_solution(8821018077273368270)
XLA Ops:
  0.6 1.4 %copy-done = bf16[1,16,53248]{2,1,0:T(8,128)(2,1)S(1)} copy-done((bf16[1,16,53248]{2,1,0:T(8,128)(2,1)S(1)}, bf16[1,16,53248]{2,1,0:T(8,128)(2,1)}, u32[]{:S(2)}) %copy-start) | copy-done | bytes 1703960
  3.4 5.0 %all-to-all-start = ((bf16[4,16,6656]{2,1,0:T(8,128)(2,1)}), bf16[4,16,6656]{2,1,0:T(8,128)(2,1)S(1)}, u32[]{:S(2)}, u32[]{:S(2)}) async-start(bf16[4,16,6656]{2,1,0:T(8,128)(2,1)} %get-tuple-element.23), calls=%async_computation | async-start | bytes 1703936 | tf_op jit(solution)/shard_map/delta_give/all_to_all | solution.py:158
  9.1 4.0 %collective-permute-start.1 = (bf16[16,1664]{1,0:T(8,128)(2,1)S(1)}, bf16[16,1664]{1,0:T(8,128)(2,1)S(1)}, u32[]{:S(2)}, u32[]{:S(2)}) collective-permute-start(bf16[16,1664]{1,0:T(8,128)(2,1)S(1)} %get-tuple-element.51), channel_id=1, source_target_pairs={{0,8},{8,72},{16,136},{24,200},{64,0},{72,64},{80,128},{88,192},{1... | collective-permute-start | bytes 159752 | tf_op jit(solution)/shard_map/q_z/ppermute | solution.py:167
  13.1 4.5 %collective-permute-start.2 = (bf16[16,1664]{1,0:T(8,128)(2,1)S(1)}, bf16[16,1664]{1,0:T(8,128)(2,1)S(1)}, u32[]{:S(2)}, u32[]{:S(2)}) collective-permute-start(bf16[16,1664]{1,0:T(8,128)(2,1)S(1)} %get-tuple-element.50), channel_id=1, source_target_pairs={{0,16},{8,80},{16,144},{24,208},{64,24},{72,88},{80,152},{88,216},... | collective-permute-start | bytes 159752 | tf_op jit(solution)/shard_map/q_z/ppermute | solution.py:167
  17.6 2.9 %collective-permute-start.3 = (bf16[16,1664]{1,0:T(8,128)(2,1)S(1)}, bf16[16,1664]{1,0:T(8,128)(2,1)S(1)}, u32[]{:S(2)}, u32[]{:S(2)}) collective-permute-start(bf16[16,1664]{1,0:T(8,128)(2,1)S(1)} %get-tuple-element.49), channel_id=1, source_target_pairs={{0,24},{8,88},{16,152},{24,216},{64,16},{72,80},{80,144},{88,208},... | collective-permute-start | bytes 159752 | tf_op jit(solution)/shard_map/q_z/ppermute | solution.py:167
  21.2 2.2 %collective-permute-done.3 = bf16[16,1664]{1,0:T(8,128)(2,1)S(1)} collective-permute-done((bf16[16,1664]{1,0:T(8,128)(2,1)S(1)}, bf16[16,1664]{1,0:T(8,128)(2,1)S(1)}, u32[]{:S(2)}, u32[]{:S(2)}) %collective-permute-start.3) | collective-permute-done | bytes 53280 | tf_op jit(solution)/shard_map/q_z/ppermute | solution.py:167
  23.5 1.5 %collective-permute-start.4 = (bf16[64,1664]{1,0:T(8,128)(2,1)S(1)}, bf16[64,1664]{1,0:T(8,128)(2,1)S(1)}, u32[]{:S(2)}, u32[]{:S(2)}) collective-permute-start(bf16[64,1664]{1,0:T(8,128)(2,1)S(1)} %pad_maximum_fusion.1.refs_0_), channel_id=1, source_target_pairs={{0,2},{2,0},{4,6},{6,4},{1,3},{3,1},{5,7},{7,5},{8,10},{10,8},{12,... | collective-permute-start | bytes 638984 | tf_op jit(solution)/shard_map/q_x/ppermute | solution.py:25
  25.0 1.8 %collective-permute-start.5 = (bf16[64,1664]{1,0:T(8,128)(2,1)S(1)}, bf16[64,1664]{1,0:T(8,128)(2,1)S(1)}, u32[]{:S(2)}, u32[]{:S(2)}) collective-permute-start(bf16[64,1664]{1,0:T(8,128)(2,1)S(1)} %pad_maximum_fusion.1.refs_0_), channel_id=1, source_target_pairs={{0,6},{2,4},{4,2},{6,0},{1,7},{3,5},{5,3},{7,1},{8,14},{10,12},{12... | collective-permute-start | bytes 638984 | tf_op jit(solution)/shard_map/q_x/ppermute | solution.py:25
  27.5 4.6 %all-to-all-start.1 = ((bf16[4,16,6656]{2,1,0:T(8,128)(2,1)}), bf16[4,16,6656]{2,1,0:T(8,128)(2,1)S(1)}, u32[]{:S(2)}, u32[]{:S(2)}) async-start(bf16[4,16,6656]{2,1,0:T(8,128)(2,1)} %get-tuple-element.26), calls=%async_computation.1 | async-start | bytes 1703936 | tf_op jit(solution)/shard_map/delta_keep/all_to_all | solution.py:158
  33.2 6.3 %collective-permute-start.15 = (bf16[2,16,6656]{2,1,0:T(8,128)(2,1)}, bf16[2,16,6656]{2,1,0:T(8,128)(2,1)}, u32[]{:S(2)}, u32[]{:S(2)}) collective-permute-start(bf16[2,16,6656]{2,1,0:T(8,128)(2,1)} %pad_maximum_fusion), channel_id=1, source_target_pairs={{0,32},{32,0},{1,33},{33,1},{2,34},{34,2},{3,35},{35,3},{4,36},{36... | collective-permute-start | bytes 1277960 | tf_op jit(solution)/shard_map/sums_zh/ppermute | solution.py:25
  40.8 5.2 %collective-permute-start.10 = (bf16[64,1664]{1,0:T(8,128)(2,1)S(1)}, bf16[64,1664]{1,0:T(8,128)(2,1)S(1)}, u32[]{:S(2)}, u32[]{:S(2)}) collective-permute-start(bf16[64,1664]{1,0:T(8,128)(2,1)S(1)} %collective-permute-done.6.refs_3_), channel_id=1, source_target_pairs={{0,1},{1,0},{2,3},{3,2},{4,5},{5,4},{6,7},{7,6},{8,9},{9,8},{10,11... | collective-permute-start | bytes 638984 | tf_op jit(solution)/shard_map/q_c/ppermute | solution.py:25
  49.7 1.5 %collective-permute-start.12 = (f32[16,128]{1,0:T(8,128)S(1)}, f32[16,128]{1,0:T(8,128)S(1)}, u32[]{:S(2)}, u32[]{:S(2)}) collective-permute-start(f32[16,128]{1,0:T(8,128)S(1)} %p_kernel.1), channel_id=1, source_target_pairs={{0,192},{64,128},{128,64},{192,0},{1,193},{65,129},{129,65},{193,1... | collective-permute-start | bytes 24584 | tf_op jit(solution)/shard_map/p_y/ppermute | solution.py:25
  51.2 1.5 %collective-permute-start.13 = (f32[16,128]{1,0:T(8,128)S(1)}, f32[16,128]{1,0:T(8,128)S(1)}, u32[]{:S(2)}, u32[]{:S(2)}) collective-permute-start(f32[16,128]{1,0:T(8,128)S(1)} %p_kernel.1), channel_id=1, source_target_pairs={{0,128},{64,192},{128,0},{192,64},{1,129},{65,193},{129,1},{193,65... | collective-permute-start | bytes 24584 | tf_op jit(solution)/shard_map/p_y/ppermute | solution.py:25
  53.8 1.8 %collective-permute-done.13 = f32[16,128]{1,0:T(8,128)S(1)} collective-permute-done((f32[16,128]{1,0:T(8,128)S(1)}, f32[16,128]{1,0:T(8,128)S(1)}, u32[]{:S(2)}, u32[]{:S(2)}) %collective-permute-start.13) | collective-permute-done | bytes 8224 | tf_op jit(solution)/shard_map/p_y/ppermute | solution.py:25
  55.6 5.8 %collective-permute-start.14 = (f32[16,128]{1,0:T(8,128)S(1)}, f32[16,128]{1,0:T(8,128)S(1)}, u32[]{:S(2)}, u32[]{:S(2)}) collective-permute-start(f32[16,128]{1,0:T(8,128)S(1)} %add_add_fusion), channel_id=1, source_target_pairs={{0,32},{32,0},{1,33},{33,1},{2,34},{34,2},{3,35},{35,3},{4,36},{36... | collective-permute-start | bytes 24584 | tf_op jit(solution)/shard_map/p_zh/ppermute | solution.py:25
  62.4 4.2 %collective-permute-start.16 = (f32[16,128]{1,0:T(8,128)S(1)}, f32[16,128]{1,0:T(8,128)S(1)}, u32[]{:S(2)}, u32[]{:S(2)}) collective-permute-start(f32[16,128]{1,0:T(8,128)S(1)} %add.79), channel_id=1, source_target_pairs={{0,1},{1,0},{2,3},{3,2},{4,5},{5,4},{6,7},{7,6},{8,9},{9,8},{10,11... | collective-permute-start | bytes 24584 | tf_op jit(solution)/shard_map/p_xc/ppermute | solution.py:25
  68.1 7.5 %all-to-all-start.2 = ((bf16[32,16,208]{2,1,0:T(8,128)(2,1)}), bf16[32,16,208]{2,1,0:T(8,128)(2,1)S(1)}, u32[]{:S(2)}, u32[]{:S(2)}) async-start(bf16[32,16,208]{2,1,0:T(8,128)(2,1)} %bitcast.55), calls=%async_computation.2 | async-start | bytes 524288 | tf_op jit(solution)/shard_map/d_cols/all_to_all | solution.py:209
  75.7 2.6 %collective-permute-start.17 = (f32[16,128]{1,0:T(8,128)S(1)}, f32[16,128]{1,0:T(8,128)S(1)}, u32[]{:S(2)}, u32[]{:S(2)}) collective-permute-start(f32[16,128]{1,0:T(8,128)S(1)} %pad_maximum_fusion.4), channel_id=1, source_target_pairs={{0,6},{2,4},{4,2},{6,0},{1,7},{3,5},{5,3},{7,1},{8,14},{10,12},{12... | collective-permute-start | bytes 24584 | tf_op jit(solution)/shard_map/p_xc/ppermute | solution.py:25
  79.8 2.9 %collective-permute-done.18 = f32[16,128]{1,0:T(8,128)S(1)} collective-permute-done((f32[16,128]{1,0:T(8,128)S(1)}, f32[16,128]{1,0:T(8,128)S(1)}, u32[]{:S(2)}, u32[]{:S(2)}) %collective-permute-start.18) | collective-permute-done | bytes 8224 | tf_op jit(solution)/shard_map/p_xc/ppermute | solution.py:25
  82.7 4.0 %all-to-all-done.2 = bf16[32,16,208]{2,1,0:T(8,128)(2,1)S(1)} async-done(((bf16[32,16,208]{2,1,0:T(8,128)(2,1)}), bf16[32,16,208]{2,1,0:T(8,128)(2,1)S(1)}, u32[]{:S(2)}, u32[]{:S(2)}) %all-to-all-start.2) | async-done | bytes 213024 | tf_op jit(solution)/shard_map/d_cols/all_to_all | solution.py:209
  88.3 1.9 %collective-permute-start.22 = (f32[4,16,128]{2,1,0:T(8,128)S(1)}, f32[4,16,128]{2,1,0:T(8,128)S(1)}, u32[]{:S(2)}, u32[]{:S(2)}) collective-permute-start(f32[4,16,128]{2,1,0:T(8,128)S(1)} %pad_maximum_fusion.3), channel_id=1, source_target_pairs={{0,8},{8,0},{16,24},{24,16},{1,9},{9,1},{17,25},{25,17},{2,10},{10... | collective-permute-start | bytes 98312 | tf_op jit(solution)/shard_map/p_zl/ppermute | solution.py:25
  90.2 1.9 %sqrt_add_fusion = (f32[16,6656]{1,0:T(8,128)S(1)}, f32[16,6656]{1,0:T(8,128)}) fusion(f32[16,6656]{1,0:T(8,128)S(1)} %get-tuple-element.42, bf16[2,16,6656]{2,1,0:T(8,128)(2,1)} %collective-permute-done.15, f32[16,6656]{1,0:T(8,128)S(1)} %copy-done.2), kind=kLoop, calls=%fused_computation.10 | loop fusion | flops 745472 | bytes 1916928 | tf_op jit(solution)/shard_map/second/add | solution.py:222
  93.3 4.4 %mid_kernel.1 = (f32[64,208]{1,0:T(8,128)}, bf16[512,208]{1,0:T(8,128)(2,1)S(1)}) custom-call(f32[256,128]{1,0:T(8,128)S(1)} %bitcast.59, bf16[512,208]{1,0:T(8,128)(2,1)S(1)} %bitcast.57), custom_call_target="tpu_custom_call" | custom-call | flops 8589934592 | bytes 1048576 | tf_op jit(solution)/shard_map/middle/mid_kernel/pallas_call | solution.py:131
  97.7 15.5 %all_to_all.20 = bf16[32,16,208]{2,1,0:T(8,128)(2,1)S(1)} all-to-all(bf16[32,16,208]{2,1,0:T(8,128)(2,1)S(1)} %bitcast.58), channel_id=1, replica_groups=mesh['y'=4,'zh'=2,'zl'=4,'x'=4,'c'=2] {'zl','x','c'}, dimensions={0} | all-to-all | bytes 425984 | tf_op jit(solution)/shard_map/approx/all_to_all | solution.py:228
  (68 shorter events, 19.1 us)
Async XLA Ops:
  3.4 20.1 %all-to-all-start = ((bf16[4,16,6656]{2,1,0:T(8,128)(2,1)}), bf16[4,16,6656]{2,1,0:T(8,128)(2,1)S(1)}, u32[]{:S(2)}, u32[]{:S(2)}) async-start(bf16[4,16,6656]{2,1,0:T(8,128)(2,1)} %get-tuple-element.23), calls=%async_computation | async-start | bytes 1703936 | tf_op jit(solution)/shard_map/delta_give/all_to_all | solution.py:158
  8.4 12.0 %collective-permute-start = (bf16[16,1664]{1,0:T(8,128)(2,1)S(1)}, bf16[16,1664]{1,0:T(8,128)(2,1)S(1)}, u32[]{:S(2)}, u32[]{:S(2)}) collective-permute-start(bf16[16,1664]{1,0:T(8,128)(2,1)S(1)} %get-tuple-element.48), channel_id=1, source_target_pairs={{0,0},{8,64},{16,128},{24,192},{64,8},{72,72},{80,136},{88,200},{1... | collective-permute-start | bytes 159752 | tf_op jit(solution)/shard_map/q_z/ppermute | solution.py:167
  9.1 11.3 %collective-permute-start.1 = (bf16[16,1664]{1,0:T(8,128)(2,1)S(1)}, bf16[16,1664]{1,0:T(8,128)(2,1)S(1)}, u32[]{:S(2)}, u32[]{:S(2)}) collective-permute-start(bf16[16,1664]{1,0:T(8,128)(2,1)S(1)} %get-tuple-element.51), channel_id=1, source_target_pairs={{0,8},{8,72},{16,136},{24,200},{64,0},{72,64},{80,128},{88,192},{1... | collective-permute-start | bytes 159752 | tf_op jit(solution)/shard_map/q_z/ppermute | solution.py:167
  13.1 8.1 %collective-permute-start.2 = (bf16[16,1664]{1,0:T(8,128)(2,1)S(1)}, bf16[16,1664]{1,0:T(8,128)(2,1)S(1)}, u32[]{:S(2)}, u32[]{:S(2)}) collective-permute-start(bf16[16,1664]{1,0:T(8,128)(2,1)S(1)} %get-tuple-element.50), channel_id=1, source_target_pairs={{0,16},{8,80},{16,144},{24,208},{64,24},{72,88},{80,152},{88,216},... | collective-permute-start | bytes 159752 | tf_op jit(solution)/shard_map/q_z/ppermute | solution.py:167
  17.6 5.9 %collective-permute-start.3 = (bf16[16,1664]{1,0:T(8,128)(2,1)S(1)}, bf16[16,1664]{1,0:T(8,128)(2,1)S(1)}, u32[]{:S(2)}, u32[]{:S(2)}) collective-permute-start(bf16[16,1664]{1,0:T(8,128)(2,1)S(1)} %get-tuple-element.49), channel_id=1, source_target_pairs={{0,24},{8,88},{16,152},{24,216},{64,16},{72,80},{80,144},{88,208},... | collective-permute-start | bytes 159752 | tf_op jit(solution)/shard_map/q_z/ppermute | solution.py:167
  23.5 16.1 %collective-permute-start.4 = (bf16[64,1664]{1,0:T(8,128)(2,1)S(1)}, bf16[64,1664]{1,0:T(8,128)(2,1)S(1)}, u32[]{:S(2)}, u32[]{:S(2)}) collective-permute-start(bf16[64,1664]{1,0:T(8,128)(2,1)S(1)} %pad_maximum_fusion.1.refs_0_), channel_id=1, source_target_pairs={{0,2},{2,0},{4,6},{6,4},{1,3},{3,1},{5,7},{7,5},{8,10},{10,8},{12,... | collective-permute-start | bytes 638984 | tf_op jit(solution)/shard_map/q_x/ppermute | solution.py:25
  25.0 14.6 %collective-permute-start.5 = (bf16[64,1664]{1,0:T(8,128)(2,1)S(1)}, bf16[64,1664]{1,0:T(8,128)(2,1)S(1)}, u32[]{:S(2)}, u32[]{:S(2)}) collective-permute-start(bf16[64,1664]{1,0:T(8,128)(2,1)S(1)} %pad_maximum_fusion.1.refs_0_), channel_id=1, source_target_pairs={{0,6},{2,4},{4,2},{6,0},{1,7},{3,5},{5,3},{7,1},{8,14},{10,12},{12... | collective-permute-start | bytes 638984 | tf_op jit(solution)/shard_map/q_x/ppermute | solution.py:25
  26.8 12.8 %collective-permute-start.6 = (bf16[64,1664]{1,0:T(8,128)(2,1)S(1)}, bf16[64,1664]{1,0:T(8,128)(2,1)S(1)}, u32[]{:S(2)}, u32[]{:S(2)}) collective-permute-start(bf16[64,1664]{1,0:T(8,128)(2,1)S(1)} %pad_maximum_fusion.1.refs_0_), channel_id=1, source_target_pairs={{0,4},{2,6},{4,0},{6,2},{1,5},{3,7},{5,1},{7,3},{8,12},{10,14},{12... | collective-permute-start | bytes 638984 | tf_op jit(solution)/shard_map/q_x/ppermute | solution.py:25
  27.5 13.3 %all-to-all-start.1 = ((bf16[4,16,6656]{2,1,0:T(8,128)(2,1)}), bf16[4,16,6656]{2,1,0:T(8,128)(2,1)S(1)}, u32[]{:S(2)}, u32[]{:S(2)}) async-start(bf16[4,16,6656]{2,1,0:T(8,128)(2,1)} %get-tuple-element.26), calls=%async_computation.1 | async-start | bytes 1703936 | tf_op jit(solution)/shard_map/delta_keep/all_to_all | solution.py:158
  33.2 19.4 %collective-permute-start.15 = (bf16[2,16,6656]{2,1,0:T(8,128)(2,1)}, bf16[2,16,6656]{2,1,0:T(8,128)(2,1)}, u32[]{:S(2)}, u32[]{:S(2)}) collective-permute-start(bf16[2,16,6656]{2,1,0:T(8,128)(2,1)} %pad_maximum_fusion), channel_id=1, source_target_pairs={{0,32},{32,0},{1,33},{33,1},{2,34},{34,2},{3,35},{35,3},{4,36},{36... | collective-permute-start | bytes 1277960 | tf_op jit(solution)/shard_map/sums_zh/ppermute | solution.py:25
  40.8 6.3 %collective-permute-start.10 = (bf16[64,1664]{1,0:T(8,128)(2,1)S(1)}, bf16[64,1664]{1,0:T(8,128)(2,1)S(1)}, u32[]{:S(2)}, u32[]{:S(2)}) collective-permute-start(bf16[64,1664]{1,0:T(8,128)(2,1)S(1)} %collective-permute-done.6.refs_3_), channel_id=1, source_target_pairs={{0,1},{1,0},{2,3},{3,2},{4,5},{5,4},{6,7},{7,6},{8,9},{9,8},{10,11... | collective-permute-start | bytes 638984 | tf_op jit(solution)/shard_map/q_c/ppermute | solution.py:25
  46.0 1.8 %collective-permute-start.8 = (bf16[64,1664]{1,0:T(8,128)(2,1)S(1)}, bf16[64,1664]{1,0:T(8,128)(2,1)S(1)}, u32[]{:S(2)}, u32[]{:S(2)}) collective-permute-start(bf16[64,1664]{1,0:T(8,128)(2,1)S(1)} %collective-permute-done.4.refs_1_), channel_id=1, source_target_pairs={{0,1},{1,0},{2,3},{3,2},{4,5},{5,4},{6,7},{7,6},{8,9},{9,8},{10,11... | collective-permute-start | bytes 638984 | tf_op jit(solution)/shard_map/q_c/ppermute | solution.py:25
  49.3 4.3 %collective-permute-start.11 = (f32[16,128]{1,0:T(8,128)S(1)}, f32[16,128]{1,0:T(8,128)S(1)}, u32[]{:S(2)}, u32[]{:S(2)}) collective-permute-start(f32[16,128]{1,0:T(8,128)S(1)} %p_kernel.1), channel_id=1, source_target_pairs={{0,64},{64,0},{128,192},{192,128},{1,65},{65,1},{129,193},{193,129... | collective-permute-start | bytes 24584 | tf_op jit(solution)/shard_map/p_y/ppermute | solution.py:25
  49.7 4.1 %collective-permute-start.12 = (f32[16,128]{1,0:T(8,128)S(1)}, f32[16,128]{1,0:T(8,128)S(1)}, u32[]{:S(2)}, u32[]{:S(2)}) collective-permute-start(f32[16,128]{1,0:T(8,128)S(1)} %p_kernel.1), channel_id=1, source_target_pairs={{0,192},{64,128},{128,64},{192,0},{1,193},{65,129},{129,65},{193,1... | collective-permute-start | bytes 24584 | tf_op jit(solution)/shard_map/p_y/ppermute | solution.py:25
  51.2 4.4 %collective-permute-start.13 = (f32[16,128]{1,0:T(8,128)S(1)}, f32[16,128]{1,0:T(8,128)S(1)}, u32[]{:S(2)}, u32[]{:S(2)}) collective-permute-start(f32[16,128]{1,0:T(8,128)S(1)} %p_kernel.1), channel_id=1, source_target_pairs={{0,128},{64,192},{128,0},{192,64},{1,129},{65,193},{129,1},{193,65... | collective-permute-start | bytes 24584 | tf_op jit(solution)/shard_map/p_y/ppermute | solution.py:25
  55.6 6.8 %collective-permute-start.14 = (f32[16,128]{1,0:T(8,128)S(1)}, f32[16,128]{1,0:T(8,128)S(1)}, u32[]{:S(2)}, u32[]{:S(2)}) collective-permute-start(f32[16,128]{1,0:T(8,128)S(1)} %add_add_fusion), channel_id=1, source_target_pairs={{0,32},{32,0},{1,33},{33,1},{2,34},{34,2},{3,35},{35,3},{4,36},{36... | collective-permute-start | bytes 24584 | tf_op jit(solution)/shard_map/p_zh/ppermute | solution.py:25
  62.4 13.2 %collective-permute-start.16 = (f32[16,128]{1,0:T(8,128)S(1)}, f32[16,128]{1,0:T(8,128)S(1)}, u32[]{:S(2)}, u32[]{:S(2)}) collective-permute-start(f32[16,128]{1,0:T(8,128)S(1)} %add.79), channel_id=1, source_target_pairs={{0,1},{1,0},{2,3},{3,2},{4,5},{5,4},{6,7},{7,6},{8,9},{9,8},{10,11... | collective-permute-start | bytes 24584 | tf_op jit(solution)/shard_map/p_xc/ppermute | solution.py:25
  68.1 18.6 %all-to-all-start.2 = ((bf16[32,16,208]{2,1,0:T(8,128)(2,1)}), bf16[32,16,208]{2,1,0:T(8,128)(2,1)S(1)}, u32[]{:S(2)}, u32[]{:S(2)}) async-start(bf16[32,16,208]{2,1,0:T(8,128)(2,1)} %bitcast.55), calls=%async_computation.2 | async-start | bytes 524288 | tf_op jit(solution)/shard_map/d_cols/all_to_all | solution.py:209
  75.7 4.1 %collective-permute-start.17 = (f32[16,128]{1,0:T(8,128)S(1)}, f32[16,128]{1,0:T(8,128)S(1)}, u32[]{:S(2)}, u32[]{:S(2)}) collective-permute-start(f32[16,128]{1,0:T(8,128)S(1)} %pad_maximum_fusion.4), channel_id=1, source_target_pairs={{0,6},{2,4},{4,2},{6,0},{1,7},{3,5},{5,3},{7,1},{8,14},{10,12},{12... | collective-permute-start | bytes 24584 | tf_op jit(solution)/shard_map/p_xc/ppermute | solution.py:25
  78.3 4.3 %collective-permute-start.18 = (f32[16,128]{1,0:T(8,128)S(1)}, f32[16,128]{1,0:T(8,128)S(1)}, u32[]{:S(2)}, u32[]{:S(2)}) collective-permute-start(f32[16,128]{1,0:T(8,128)S(1)} %pad_maximum_fusion.4), channel_id=1, source_target_pairs={{0,4},{2,6},{4,0},{6,2},{1,5},{3,7},{5,1},{7,3},{8,12},{10,14},{12... | collective-permute-start | bytes 24584 | tf_op jit(solution)/shard_map/p_xc/ppermute | solution.py:25
  78.9 3.8 %collective-permute-start.19 = (f32[16,128]{1,0:T(8,128)S(1)}, f32[16,128]{1,0:T(8,128)S(1)}, u32[]{:S(2)}, u32[]{:S(2)}) collective-permute-start(f32[16,128]{1,0:T(8,128)S(1)} %pad_maximum_fusion.4), channel_id=1, source_target_pairs={{0,2},{2,0},{4,6},{6,4},{1,3},{3,1},{5,7},{7,5},{8,10},{10,8},{12,... | collective-permute-start | bytes 24584 | tf_op jit(solution)/shard_map/p_xc/ppermute | solution.py:25
  86.7 5.4 %collective-permute-start.20 = (f32[4,16,128]{2,1,0:T(8,128)S(1)}, f32[4,16,128]{2,1,0:T(8,128)S(1)}, u32[]{:S(2)}, u32[]{:S(2)}) collective-permute-start(f32[4,16,128]{2,1,0:T(8,128)S(1)} %pad_maximum_fusion.3), channel_id=1, source_target_pairs={{0,24},{8,16},{16,8},{24,0},{1,25},{9,17},{17,9},{25,1},{2,26},{10... | collective-permute-start | bytes 98312 | tf_op jit(solution)/shard_map/p_zl/ppermute | solution.py:25
  87.9 5.3 %collective-permute-start.21 = (f32[4,16,128]{2,1,0:T(8,128)S(1)}, f32[4,16,128]{2,1,0:T(8,128)S(1)}, u32[]{:S(2)}, u32[]{:S(2)}) collective-permute-start(f32[4,16,128]{2,1,0:T(8,128)S(1)} %pad_maximum_fusion.3), channel_id=1, source_target_pairs={{0,16},{8,24},{16,0},{24,8},{1,17},{9,25},{17,1},{25,9},{2,18},{10... | collective-permute-start | bytes 98312 | tf_op jit(solution)/shard_map/p_zl/ppermute | solution.py:25
  88.3 4.9 %collective-permute-start.22 = (f32[4,16,128]{2,1,0:T(8,128)S(1)}, f32[4,16,128]{2,1,0:T(8,128)S(1)}, u32[]{:S(2)}, u32[]{:S(2)}) collective-permute-start(f32[4,16,128]{2,1,0:T(8,128)S(1)} %pad_maximum_fusion.3), channel_id=1, source_target_pairs={{0,8},{8,0},{16,24},{24,16},{1,9},{9,1},{17,25},{25,17},{2,10},{10... | collective-permute-start | bytes 98312 | tf_op jit(solution)/shard_map/p_zl/ppermute | solution.py:25
  (6 other events, 55.6 us)

commit v3 on v2

--- a/solution.py
+++ b/solution.py
@@ -114,18 +114,17 @@
     return a[:, n:] * (1.0 / jnp.sqrt(scale))
 
 
-def mid_kernel(p_ref, came, q_out, approx_out):
-    half, rank = came.shape[0], 64
-    pairs = p_ref[...].reshape(16, half // 32, 2 * rank)
-    p = jnp.concatenate([pairs[:, :, :rank], pairs[:, :, rank:]], axis=1).reshape(half, rank)
+def mid_kernel(came, q_out, approx_out):
+    rank, span = q_out.shape
+    p = came[:, 256 : 256 + rank].astype(f32) + came[:, 256 + rank :].astype(f32)
     inverse = inverse_factor(dot(p, p, ((0,), (0,)), HIGHEST))
     p_orth = dot(p, inverse, ((1,), (1,)), HIGHEST).astype(bf16)
-    q_t = dot(p_orth, came[...], ((0,), (0,))) / REPS
+    q_t = dot(p_orth, came[:, :span], ((0,), (0,))) / REPS
     q_out[...] = q_t
     approx_out[...] = dot(p_orth.astype(f32), q_t, ((1,), (0,)), HIGHEST).astype(bf16)
 
 
-def middle(p_sum, came, span):
+def middle(came, span):
     vmem = pl.BlockSpec(memory_space=pltpu.VMEM)
     rows = came.shape[0]
     return pl.pallas_call(
@@ -134,12 +133,12 @@
             jax.ShapeDtypeStruct((64, span), f32),
             jax.ShapeDtypeStruct((rows, span), bf16),
         ),
-        in_specs=[vmem, vmem],
+        in_specs=[vmem],
         out_specs=(vmem, vmem),
         compiler_params=pltpu.CompilerParams(vmem_limit_bytes=32 * 2**20),
         cost_estimate=pl.CostEstimate(flops=2**33, bytes_accessed=2**20, transcendentals=0),
         name="mid_kernel",
-    )(p_sum, came)
+    )(came)
 
 
 def body(delta, q_start, first_moment, second_moment):
@@ -203,26 +202,22 @@
     with jax.named_scope("p_zh"):
         p_part = p_part + swap(p_part, "zh", 1)
         p_part, d_came = lax.optimization_barrier((p_part, d_came))
-    with jax.named_scope("d_cols"):
+    with jax.named_scope("send"):
         d_rows = (d_keep + d_came.astype(f32)).astype(bf16)
         d_rows = d_rows.reshape(rows, 32, narrow).transpose(1, 0, 2)
-        came = lax.all_to_all(d_rows, ROW, 0, 0, tiled=True)
-    with jax.named_scope("p_xc"):
-        other = swap(p_part, "c", 1)
-        pair = jnp.where(c == 0, p_part[:, :rank], other[:, :rank]), jnp.where(c == 0, other[:, :rank], p_part[:, :rank])
-        pair = jnp.concatenate(pair, axis=1)
-        p_x = jnp.stack(in_order([pair] + [swap(pair, "x", k) for k in (1, 2, 3)], x))
-    with jax.named_scope("p_zl"):
-        p_x, came = lax.optimization_barrier((p_x, came))
-        p_z = [p_x] + [swap(p_x, "zl", k) for k in (1, 2, 3)]
-        p_sum = jnp.stack(in_order(p_z, lax.axis_index("zl"))).reshape(16 * rows, 2 * rank)
+        d_rows = jnp.pad(d_rows, ((0, 0), (0, 0), (0, 256 - narrow)))
+        p_rows = p_part[:, :rank]
+        high = lax.reduce_precision(p_rows, 8, 7)
+        p_rows = jnp.concatenate([high, p_rows - high], axis=1).astype(bf16)
+        p_rows = jnp.broadcast_to(p_rows[None], (32, rows, 2 * rank))
+        came = lax.all_to_all(jnp.concatenate([d_rows, p_rows], axis=2), ROW, 0, 0, tiled=True)
     with jax.named_scope("second"):
         mean_square = (s_keep + s_came.astype(f32)) / REPS
         new_second = beta_second * second_moment + (1.0 - beta_second) * mean_square
         below = jnp.sqrt(new_second * fix_second) + epsilon
         came, new_second, below = lax.optimization_barrier((came, new_second, below))
     with jax.named_scope("middle"):
-        q_t, approx_cols = middle(p_sum, came.reshape(32 * rows, narrow), narrow)
+        q_t, approx_cols = middle(came.reshape(32 * rows, 256 + 2 * rank), narrow)
         q_new = q_t.T
     with jax.named_scope("approx"):
         approx = lax.all_to_all(

time: 115 us -> 110 us (0.957)
  starting transfers between devices: 65.3 us -> 55.7 us
  waiting for transfers between devices: 17 us -> 22.1 us
    ppermute x19 -> x12, starting transfers between devices: 36.2 us -> 25.4 us  [swap(): lax.ppermute(x, axis, [(i, i ^ bits) for i in range(lax.axis_size(axis))])]
    all_to_all x1, waiting for transfers between devices: 4.01 us -> 11.9 us  [body(): lax.all_to_all(jnp.concatenate([d_rows, p_rows], axis=2), ROW, 0, 0, tile...]
    ppermute x19 -> x12, waiting for transfers between devices: 8.85 us -> 4.02 us  [swap(): lax.ppermute(x, axis, [(i, i ^ bits) for i in range(lax.axis_size(axis))])]
    all_to_all x1, starting transfers between devices: 7.51 us -> 11.3 us  [body(): lax.all_to_all(jnp.concatenate([d_rows, p_rows], axis=2), ROW, 0, 0, tile...]
    ppermute x4, starting transfers between devices: 12 us -> 9.73 us  [body(): lax.ppermute(q_t[quarter * s:quarter * (s + 1)], ('y', 'zl'), [(a * 4 + b...]
    ppermute x4, waiting for transfers between devices: 3.03 us -> 4.76 us  [body(): lax.ppermute(q_t[quarter * s:quarter * (s + 1)], ('y', 'zl'), [(a * 4 + b...]
  transfers between devices with their start and end apart: 26 -> 19, of which waited for: 14 -> 11; matrix products, arithmetic and copies ran while one was open for 5% -> 4% of each run, Pallas kernels for 1% -> 1%
where the time goes in v3:
time: 110 us
  starting transfers between devices  55.7 us (51%)
  waiting for transfers between devices  22.1 us (20%)
  blocking collectives  15 us (14%)
  Pallas kernels  6.9 us (6%)
  other arithmetic  5.33 us (5%)
  local copies, waits for them, and re-layouts  3.95 us (4%)
    ppermute x12, starting transfers between devices, swap(): lax.ppermute(x, axis, [(i, i ^ bits) for i in range(lax.axis_size(axis))])  25.4 us
    all_to_all x1, blocking collectives, body(): lax.all_to_all(approx_cols.reshape(32, rows, narrow), ROW, 0, 0, tiled=True)  15 us
    all_to_all x1, waiting for transfers between devices, body(): lax.all_to_all(jnp.concatenate([d_rows, p_rows], axis=2), ROW, 0, 0, tile...  11.9 us
    all_to_all x1, starting transfers between devices, body(): lax.all_to_all(jnp.concatenate([d_rows, p_rows], axis=2), ROW, 0, 0, tile...  11.3 us
    ppermute x4, starting transfers between devices, body(): lax.ppermute(q_t[quarter * s:quarter * (s + 1)], ('y', 'zl'), [(a * 4 + b...  9.73 us
    all_to_all x2, starting transfers between devices, along_y(): return lax.all_to_all(a, 'y', 0, 0, tiled=True)  9.28 us
    ppermute x4, waiting for transfers between devices, body(): lax.ppermute(q_t[quarter * s:quarter * (s + 1)], ('y', 'zl'), [(a * 4 + b...  4.76 us
    pallas_call x1, Pallas kernels, middle(): pl.pallas_call(mid_kernel, out_shape=(jax.ShapeDtypeStruct((64, span), f3...  4.39 us
  transfers between devices with their start and end apart: 19, of which 11 were waited for; matrix products, arithmetic and copies ran while one was open for 4% of the time, Pallas kernels for 1%

profile of v3, /device:TPU:1, one launch (start us, length us, event | category | flops | bytes accessed | tf_op | source)
XLA Modules:
  0.0 109.8 jit_solution(6422798965515697700)
XLA Ops:
  0.6 1.4 %copy-done = bf16[1,16,53248]{2,1,0:T(8,128)(2,1)S(1)} copy-done((bf16[1,16,53248]{2,1,0:T(8,128)(2,1)S(1)}, bf16[1,16,53248]{2,1,0:T(8,128)(2,1)}, u32[]{:S(2)}) %copy-start) | copy-done | bytes 1703960
  2.1 1.3 %split_kernel.1 = (bf16[4,16,6656]{2,1,0:T(8,128)(2,1)}, bf16[4,16,6656]{2,1,0:T(8,128)(2,1)}) custom-call(s32[1]{0:T(128)} %bitcast.1.zh, bf16[16,53248]{1,0:T(8,128)(2,1)S(1)} %bitcast.39), custom_call_target="tpu_custom_call" | custom-call | bytes 4194304 | tf_op jit(solution)/shard_map/split_kernel/pallas_call | solution.py:53
  3.4 5.0 %all-to-all-start = ((bf16[4,16,6656]{2,1,0:T(8,128)(2,1)}), bf16[4,16,6656]{2,1,0:T(8,128)(2,1)S(1)}, u32[]{:S(2)}, u32[]{:S(2)}) async-start(bf16[4,16,6656]{2,1,0:T(8,128)(2,1)} %get-tuple-element.21), calls=%async_computation | async-start | bytes 1703936 | tf_op jit(solution)/shard_map/delta_give/all_to_all | solution.py:157
  9.1 7.0 %collective-permute-start.3 = (bf16[16,1664]{1,0:T(8,128)(2,1)S(1)}, bf16[16,1664]{1,0:T(8,128)(2,1)S(1)}, u32[]{:S(2)}, u32[]{:S(2)}) collective-permute-start(bf16[16,1664]{1,0:T(8,128)(2,1)S(1)} %get-tuple-element.45), channel_id=1, source_target_pairs={{0,24},{8,88},{16,152},{24,216},{64,16},{72,80},{80,144},{88,208},... | collective-permute-start | bytes 159752 | tf_op jit(solution)/shard_map/q_z/ppermute | solution.py:166
  16.1 2.1 %collective-permute-start.2 = (bf16[16,1664]{1,0:T(8,128)(2,1)S(1)}, bf16[16,1664]{1,0:T(8,128)(2,1)S(1)}, u32[]{:S(2)}, u32[]{:S(2)}) collective-permute-start(bf16[16,1664]{1,0:T(8,128)(2,1)S(1)} %get-tuple-element.46), channel_id=1, source_target_pairs={{0,16},{8,80},{16,144},{24,208},{64,24},{72,88},{80,152},{88,216},... | collective-permute-start | bytes 159752 | tf_op jit(solution)/shard_map/q_z/ppermute | solution.py:166
  18.2 4.7 %collective-permute-done.3 = bf16[16,1664]{1,0:T(8,128)(2,1)S(1)} collective-permute-done((bf16[16,1664]{1,0:T(8,128)(2,1)S(1)}, bf16[16,1664]{1,0:T(8,128)(2,1)S(1)}, u32[]{:S(2)}, u32[]{:S(2)}) %collective-permute-start.3) | collective-permute-done | bytes 53280 | tf_op jit(solution)/shard_map/q_z/ppermute | solution.py:166
  23.0 3.6 %collective-permute-start.6 = (bf16[64,1664]{1,0:T(8,128)(2,1)S(1)}, bf16[64,1664]{1,0:T(8,128)(2,1)S(1)}, u32[]{:S(2)}, u32[]{:S(2)}) collective-permute-start(bf16[64,1664]{1,0:T(8,128)(2,1)S(1)} %pad_maximum_fusion.1.refs_0_), channel_id=1, source_target_pairs={{0,4},{2,6},{4,0},{6,2},{1,5},{3,7},{5,1},{7,3},{8,12},{10,14},{12... | collective-permute-start | bytes 638984 | tf_op jit(solution)/shard_map/q_x/ppermute | solution.py:25
  27.4 4.3 %all-to-all-start.1 = ((bf16[4,16,6656]{2,1,0:T(8,128)(2,1)}), bf16[4,16,6656]{2,1,0:T(8,128)(2,1)S(1)}, u32[]{:S(2)}, u32[]{:S(2)}) async-start(bf16[4,16,6656]{2,1,0:T(8,128)(2,1)} %get-tuple-element.24), calls=%async_computation.1 | async-start | bytes 1703936 | tf_op jit(solution)/shard_map/delta_keep/all_to_all | solution.py:157
  32.9 6.0 %collective-permute-start.15 = (bf16[2,16,6656]{2,1,0:T(8,128)(2,1)}, bf16[2,16,6656]{2,1,0:T(8,128)(2,1)}, u32[]{:S(2)}, u32[]{:S(2)}) collective-permute-start(bf16[2,16,6656]{2,1,0:T(8,128)(2,1)} %pad_maximum_fusion), channel_id=1, source_target_pairs={{0,32},{32,0},{1,33},{33,1},{2,34},{34,2},{3,35},{35,3},{4,36},{36... | collective-permute-start | bytes 1277960 | tf_op jit(solution)/shard_map/sums_zh/ppermute | solution.py:25
  39.0 1.4 %all-to-all-done.1.refs_9_ = bf16[4,16,6656]{2,1,0:T(8,128)(2,1)S(1)} async-done(((bf16[4,16,6656]{2,1,0:T(8,128)(2,1)}), bf16[4,16,6656]{2,1,0:T(8,128)(2,1)S(1)}, u32[]{:S(2)}, u32[]{:S(2)}) %all-to-all-start.1) | async-done | bytes 852000 | tf_op jit(solution)/shard_map/delta_keep/all_to_all | solution.py:157
  40.4 5.2 %collective-permute-start.7 = (bf16[64,1664]{1,0:T(8,128)(2,1)S(1)}, bf16[64,1664]{1,0:T(8,128)(2,1)S(1)}, u32[]{:S(2)}, u32[]{:S(2)}) collective-permute-start(bf16[64,1664]{1,0:T(8,128)(2,1)S(1)} %pad_maximum_fusion.1.refs_0_), channel_id=1, source_target_pairs={{0,1},{1,0},{2,3},{3,2},{4,5},{5,4},{6,7},{7,6},{8,9},{9,8},{10,11... | collective-permute-start | bytes 638984 | tf_op jit(solution)/shard_map/q_c/ppermute | solution.py:25
  47.7 1.2 %p_kernel.1 = f32[16,128]{1,0:T(8,128)S(1)} custom-call(s32[2,8]{1,0:T(2,128)S(1)} %pad_add_fusion.places, bf16[64,1664]{1,0:T(8,128)(2,1)S(1)} %pad_maximum_fusion.1.refs_0_, bf16[64,1664]{1,0:T(8,128)(2,1)S(1)} %collective-permute-done.4.refs_1_, bf16[64,1664]{1,0:T(8,128)(2,1)S(1)} %collective-permute-done.5.refs_2_, ...), custom_call_target="tpu_custom_call" | custom-call | flops 134217728 | bytes 3145728 | tf_op jit(solution)/shard_map/p_part/p_kernel/pallas_call | solution.py:80
  48.9 1.1 %collective-permute-start.13 = (f32[16,128]{1,0:T(8,128)S(1)}, f32[16,128]{1,0:T(8,128)S(1)}, u32[]{:S(2)}, u32[]{:S(2)}) collective-permute-start(f32[16,128]{1,0:T(8,128)S(1)} %p_kernel.1), channel_id=1, source_target_pairs={{0,128},{64,192},{128,0},{192,64},{1,129},{65,193},{129,1},{193,65... | collective-permute-start | bytes 24584 | tf_op jit(solution)/shard_map/p_y/ppermute | solution.py:25
  50.1 1.6 %collective-permute-start.12 = (f32[16,128]{1,0:T(8,128)S(1)}, f32[16,128]{1,0:T(8,128)S(1)}, u32[]{:S(2)}, u32[]{:S(2)}) collective-permute-start(f32[16,128]{1,0:T(8,128)S(1)} %p_kernel.1), channel_id=1, source_target_pairs={{0,192},{64,128},{128,64},{192,0},{1,193},{65,129},{129,65},{193,1... | collective-permute-start | bytes 24584 | tf_op jit(solution)/shard_map/p_y/ppermute | solution.py:25
  51.7 0.9 slice_bitcast_fusion.1
  53.0 1.1 collective-permute-done.12
  54.2 6.4 %collective-permute-start.14 = (f32[16,128]{1,0:T(8,128)S(1)}, f32[16,128]{1,0:T(8,128)S(1)}, u32[]{:S(2)}, u32[]{:S(2)}) collective-permute-start(f32[16,128]{1,0:T(8,128)S(1)} %add_add_fusion), channel_id=1, source_target_pairs={{0,32},{32,0},{1,33},{33,1},{2,34},{34,2},{3,35},{35,3},{4,36},{36... | collective-permute-start | bytes 24584 | tf_op jit(solution)/shard_map/p_zh/ppermute | solution.py:25
  60.9 1.1 %collective-permute-done.14 = f32[16,128]{1,0:T(8,128)S(1)} collective-permute-done((f32[16,128]{1,0:T(8,128)S(1)}, f32[16,128]{1,0:T(8,128)S(1)}, u32[]{:S(2)}, u32[]{:S(2)}) %collective-permute-start.14) | collective-permute-done | bytes 8224 | tf_op jit(solution)/shard_map/p_zh/ppermute | solution.py:25
  63.7 11.3 %all-to-all-start.2 = ((bf16[32,16,384]{2,1,0:T(8,128)(2,1)}), bf16[32,16,384]{2,1,0:T(8,128)(2,1)S(1)}, u32[]{:S(2)}, u32[]{:S(2)}) async-start(bf16[32,16,384]{2,1,0:T(8,128)(2,1)} %fusion.4), calls=%async_computation.2 | async-start | bytes 786432 | tf_op jit(solution)/shard_map/send/all_to_all | solution.py:213
  75.0 1.9 %sqrt_add_fusion = (f32[16,6656]{1,0:T(8,128)S(1)}, f32[16,6656]{1,0:T(8,128)}) fusion(f32[16,6656]{1,0:T(8,128)S(1)} %get-tuple-element.38, bf16[2,16,6656]{2,1,0:T(8,128)(2,1)} %collective-permute-done.15, f32[16,6656]{1,0:T(8,128)S(1)} %copy-done.2), kind=kLoop, calls=%fused_computation.12 | loop fusion | flops 745472 | bytes 1916928 | tf_op jit(solution)/shard_map/second/add | solution.py:217
  76.9 11.9 %all-to-all-done.2 = bf16[32,16,384]{2,1,0:T(8,128)(2,1)S(1)} async-done(((bf16[32,16,384]{2,1,0:T(8,128)(2,1)}), bf16[32,16,384]{2,1,0:T(8,128)(2,1)S(1)}, u32[]{:S(2)}, u32[]{:S(2)}) %all-to-all-start.2) | async-done | bytes 393248 | tf_op jit(solution)/shard_map/send/all_to_all | solution.py:213
  88.8 4.4 %mid_kernel.1 = (f32[64,208]{1,0:T(8,128)}, bf16[512,208]{1,0:T(8,128)(2,1)S(1)}) custom-call(bf16[512,384]{1,0:T(8,128)(2,1)S(1)} %bitcast.40), custom_call_target="tpu_custom_call" | custom-call | flops 8589934592 | bytes 1048576 | tf_op jit(solution)/shard_map/middle/mid_kernel/pallas_call | solution.py:130
  93.2 15.0 %all_to_all.20 = bf16[32,16,208]{2,1,0:T(8,128)(2,1)S(1)} all-to-all(bf16[32,16,208]{2,1,0:T(8,128)(2,1)S(1)} %bitcast.41), channel_id=1, replica_groups=mesh['y'=4,'zh'=2,'zl'=4,'x'=4,'c'=2] {'zl','x','c'}, dimensions={0} | all-to-all | bytes 425984 | tf_op jit(solution)/shard_map/approx/all_to_all | solution.py:223
  108.8 1.0 multiply_divide_fusion
  (52 shorter events, 7.9 us)
Async XLA Ops:
  0.6 1.5 %copy-start = (bf16[1,16,53248]{2,1,0:T(8,128)(2,1)S(1)}, bf16[1,16,53248]{2,1,0:T(8,128)(2,1)}, u32[]{:S(2)}) copy-start(bf16[1,16,53248]{2,1,0:T(8,128)(2,1)} %param.4) | copy-start | bytes 5111812
  2.1 6.3 %copy-start.3 = (bf16[1664,64]{0,1:T(8,128)(2,1)S(1)}, bf16[1664,64]{0,1:T(8,128)(2,1)}, u32[]{:S(2)}) copy-start(bf16[1664,64]{0,1:T(8,128)(2,1)} %param.5) | copy-start | bytes 638980
  3.4 19.6 %all-to-all-start = ((bf16[4,16,6656]{2,1,0:T(8,128)(2,1)}), bf16[4,16,6656]{2,1,0:T(8,128)(2,1)S(1)}, u32[]{:S(2)}, u32[]{:S(2)}) async-start(bf16[4,16,6656]{2,1,0:T(8,128)(2,1)} %get-tuple-element.21), calls=%async_computation | async-start | bytes 1703936 | tf_op jit(solution)/shard_map/delta_give/all_to_all | solution.py:157
  8.4 9.7 %collective-permute-start = (bf16[16,1664]{1,0:T(8,128)(2,1)S(1)}, bf16[16,1664]{1,0:T(8,128)(2,1)S(1)}, u32[]{:S(2)}, u32[]{:S(2)}) collective-permute-start(bf16[16,1664]{1,0:T(8,128)(2,1)S(1)} %get-tuple-element.44), channel_id=1, source_target_pairs={{0,0},{8,64},{16,128},{24,192},{64,8},{72,72},{80,136},{88,200},{1... | collective-permute-start | bytes 159752 | tf_op jit(solution)/shard_map/q_z/ppermute | solution.py:166
  9.1 13.8 %collective-permute-start.3 = (bf16[16,1664]{1,0:T(8,128)(2,1)S(1)}, bf16[16,1664]{1,0:T(8,128)(2,1)S(1)}, u32[]{:S(2)}, u32[]{:S(2)}) collective-permute-start(bf16[16,1664]{1,0:T(8,128)(2,1)S(1)} %get-tuple-element.45), channel_id=1, source_target_pairs={{0,24},{8,88},{16,152},{24,216},{64,16},{72,80},{80,144},{88,208},... | collective-permute-start | bytes 159752 | tf_op jit(solution)/shard_map/q_z/ppermute | solution.py:166
  16.1 6.8 %collective-permute-start.2 = (bf16[16,1664]{1,0:T(8,128)(2,1)S(1)}, bf16[16,1664]{1,0:T(8,128)(2,1)S(1)}, u32[]{:S(2)}, u32[]{:S(2)}) collective-permute-start(bf16[16,1664]{1,0:T(8,128)(2,1)S(1)} %get-tuple-element.46), channel_id=1, source_target_pairs={{0,16},{8,80},{16,144},{24,208},{64,24},{72,88},{80,152},{88,216},... | collective-permute-start | bytes 159752 | tf_op jit(solution)/shard_map/q_z/ppermute | solution.py:166
  18.2 4.8 %collective-permute-start.1 = (bf16[16,1664]{1,0:T(8,128)(2,1)S(1)}, bf16[16,1664]{1,0:T(8,128)(2,1)S(1)}, u32[]{:S(2)}, u32[]{:S(2)}) collective-permute-start(bf16[16,1664]{1,0:T(8,128)(2,1)S(1)} %get-tuple-element.47), channel_id=1, source_target_pairs={{0,8},{8,72},{16,136},{24,200},{64,0},{72,64},{80,128},{88,192},{1... | collective-permute-start | bytes 159752 | tf_op jit(solution)/shard_map/q_z/ppermute | solution.py:166
  23.0 16.0 %collective-permute-start.6 = (bf16[64,1664]{1,0:T(8,128)(2,1)S(1)}, bf16[64,1664]{1,0:T(8,128)(2,1)S(1)}, u32[]{:S(2)}, u32[]{:S(2)}) collective-permute-start(bf16[64,1664]{1,0:T(8,128)(2,1)S(1)} %pad_maximum_fusion.1.refs_0_), channel_id=1, source_target_pairs={{0,4},{2,6},{4,0},{6,2},{1,5},{3,7},{5,1},{7,3},{8,12},{10,14},{12... | collective-permute-start | bytes 638984 | tf_op jit(solution)/shard_map/q_x/ppermute | solution.py:25
  26.6 12.4 %collective-permute-start.5 = (bf16[64,1664]{1,0:T(8,128)(2,1)S(1)}, bf16[64,1664]{1,0:T(8,128)(2,1)S(1)}, u32[]{:S(2)}, u32[]{:S(2)}) collective-permute-start(bf16[64,1664]{1,0:T(8,128)(2,1)S(1)} %pad_maximum_fusion.1.refs_0_), channel_id=1, source_target_pairs={{0,6},{2,4},{4,2},{6,0},{1,7},{3,5},{5,3},{7,1},{8,14},{10,12},{12... | collective-permute-start | bytes 638984 | tf_op jit(solution)/shard_map/q_x/ppermute | solution.py:25
  27.4 11.6 %collective-permute-start.4 = (bf16[64,1664]{1,0:T(8,128)(2,1)S(1)}, bf16[64,1664]{1,0:T(8,128)(2,1)S(1)}, u32[]{:S(2)}, u32[]{:S(2)}) collective-permute-start(bf16[64,1664]{1,0:T(8,128)(2,1)S(1)} %pad_maximum_fusion.1.refs_0_), channel_id=1, source_target_pairs={{0,2},{2,0},{4,6},{6,4},{1,3},{3,1},{5,7},{7,5},{8,10},{10,8},{12,... | collective-permute-start | bytes 638984 | tf_op jit(solution)/shard_map/q_x/ppermute | solution.py:25
  27.4 13.0 %all-to-all-start.1 = ((bf16[4,16,6656]{2,1,0:T(8,128)(2,1)}), bf16[4,16,6656]{2,1,0:T(8,128)(2,1)S(1)}, u32[]{:S(2)}, u32[]{:S(2)}) async-start(bf16[4,16,6656]{2,1,0:T(8,128)(2,1)} %get-tuple-element.24), calls=%async_computation.1 | async-start | bytes 1703936 | tf_op jit(solution)/shard_map/delta_keep/all_to_all | solution.py:157
  32.9 18.9 %collective-permute-start.15 = (bf16[2,16,6656]{2,1,0:T(8,128)(2,1)}, bf16[2,16,6656]{2,1,0:T(8,128)(2,1)}, u32[]{:S(2)}, u32[]{:S(2)}) collective-permute-start(bf16[2,16,6656]{2,1,0:T(8,128)(2,1)} %pad_maximum_fusion), channel_id=1, source_target_pairs={{0,32},{32,0},{1,33},{33,1},{2,34},{34,2},{3,35},{35,3},{4,36},{36... | collective-permute-start | bytes 1277960 | tf_op jit(solution)/shard_map/sums_zh/ppermute | solution.py:25
  40.4 6.3 %collective-permute-start.7 = (bf16[64,1664]{1,0:T(8,128)(2,1)S(1)}, bf16[64,1664]{1,0:T(8,128)(2,1)S(1)}, u32[]{:S(2)}, u32[]{:S(2)}) collective-permute-start(bf16[64,1664]{1,0:T(8,128)(2,1)S(1)} %pad_maximum_fusion.1.refs_0_), channel_id=1, source_target_pairs={{0,1},{1,0},{2,3},{3,2},{4,5},{5,4},{6,7},{7,6},{8,9},{9,8},{10,11... | collective-permute-start | bytes 638984 | tf_op jit(solution)/shard_map/q_c/ppermute | solution.py:25
  45.6 1.5 %collective-permute-start.8 = (bf16[64,1664]{1,0:T(8,128)(2,1)S(1)}, bf16[64,1664]{1,0:T(8,128)(2,1)S(1)}, u32[]{:S(2)}, u32[]{:S(2)}) collective-permute-start(bf16[64,1664]{1,0:T(8,128)(2,1)S(1)} %collective-permute-done.4.refs_1_), channel_id=1, source_target_pairs={{0,1},{1,0},{2,3},{3,2},{4,5},{5,4},{6,7},{7,6},{8,9},{9,8},{10,11... | collective-permute-start | bytes 638984 | tf_op jit(solution)/shard_map/q_c/ppermute | solution.py:25
  45.6 1.8 %collective-permute-start.9 = (bf16[64,1664]{1,0:T(8,128)(2,1)S(1)}, bf16[64,1664]{1,0:T(8,128)(2,1)S(1)}, u32[]{:S(2)}, u32[]{:S(2)}) collective-permute-start(bf16[64,1664]{1,0:T(8,128)(2,1)S(1)} %collective-permute-done.5.refs_2_), channel_id=1, source_target_pairs={{0,1},{1,0},{2,3},{3,2},{4,5},{5,4},{6,7},{7,6},{8,9},{9,8},{10,11... | collective-permute-start | bytes 638984 | tf_op jit(solution)/shard_map/q_c/ppermute | solution.py:25
  46.1 1.6 %collective-permute-start.10 = (bf16[64,1664]{1,0:T(8,128)(2,1)S(1)}, bf16[64,1664]{1,0:T(8,128)(2,1)S(1)}, u32[]{:S(2)}, u32[]{:S(2)}) collective-permute-start(bf16[64,1664]{1,0:T(8,128)(2,1)S(1)} %collective-permute-done.6.refs_3_), channel_id=1, source_target_pairs={{0,1},{1,0},{2,3},{3,2},{4,5},{5,4},{6,7},{7,6},{8,9},{9,8},{10,11... | collective-permute-start | bytes 638984 | tf_op jit(solution)/shard_map/q_c/ppermute | solution.py:25
  48.9 4.1 %collective-permute-start.13 = (f32[16,128]{1,0:T(8,128)S(1)}, f32[16,128]{1,0:T(8,128)S(1)}, u32[]{:S(2)}, u32[]{:S(2)}) collective-permute-start(f32[16,128]{1,0:T(8,128)S(1)} %p_kernel.1), channel_id=1, source_target_pairs={{0,128},{64,192},{128,0},{192,64},{1,129},{65,193},{129,1},{193,65... | collective-permute-start | bytes 24584 | tf_op jit(solution)/shard_map/p_y/ppermute | solution.py:25
  50.1 4.0 %collective-permute-start.12 = (f32[16,128]{1,0:T(8,128)S(1)}, f32[16,128]{1,0:T(8,128)S(1)}, u32[]{:S(2)}, u32[]{:S(2)}) collective-permute-start(f32[16,128]{1,0:T(8,128)S(1)} %p_kernel.1), channel_id=1, source_target_pairs={{0,192},{64,128},{128,64},{192,0},{1,193},{65,129},{129,65},{193,1... | collective-permute-start | bytes 24584 | tf_op jit(solution)/shard_map/p_y/ppermute | solution.py:25
  51.7 2.5 %collective-permute-start.11 = (f32[16,128]{1,0:T(8,128)S(1)}, f32[16,128]{1,0:T(8,128)S(1)}, u32[]{:S(2)}, u32[]{:S(2)}) collective-permute-start(f32[16,128]{1,0:T(8,128)S(1)} %p_kernel.1), channel_id=1, source_target_pairs={{0,64},{64,0},{128,192},{192,128},{1,65},{65,1},{129,193},{193,129... | collective-permute-start | bytes 24584 | tf_op jit(solution)/shard_map/p_y/ppermute | solution.py:25
  54.2 7.8 %collective-permute-start.14 = (f32[16,128]{1,0:T(8,128)S(1)}, f32[16,128]{1,0:T(8,128)S(1)}, u32[]{:S(2)}, u32[]{:S(2)}) collective-permute-start(f32[16,128]{1,0:T(8,128)S(1)} %add_add_fusion), channel_id=1, source_target_pairs={{0,32},{32,0},{1,33},{33,1},{2,34},{34,2},{3,35},{35,3},{4,36},{36... | collective-permute-start | bytes 24584 | tf_op jit(solution)/shard_map/p_zh/ppermute | solution.py:25
  62.0 13.0 %copy-start.2 = (f32[16,6656]{1,0:T(8,128)S(1)}, f32[16,6656]{1,0:T(8,128)}, u32[]{:S(2)}) copy-start(f32[16,6656]{1,0:T(8,128)} %param.7) | copy-start | bytes 1277956
  63.7 25.1 %all-to-all-start.2 = ((bf16[32,16,384]{2,1,0:T(8,128)(2,1)}), bf16[32,16,384]{2,1,0:T(8,128)(2,1)S(1)}, u32[]{:S(2)}, u32[]{:S(2)}) async-start(bf16[32,16,384]{2,1,0:T(8,128)(2,1)} %fusion.4), calls=%async_computation.2 | async-start | bytes 786432 | tf_op jit(solution)/shard_map/send/all_to_all | solution.py:213
  93.2 15.7 %copy-start.1 = (f32[16,6656]{1,0:T(8,128)S(1)}, f32[16,6656]{1,0:T(8,128)}, u32[]{:S(2)}) copy-start(f32[16,6656]{1,0:T(8,128)} %param.6) | copy-start | bytes 1277956

commit v4 on v3

--- a/solution.py
+++ b/solution.py
@@ -121,7 +121,10 @@
     p_orth = dot(p, inverse, ((1,), (1,)), HIGHEST).astype(bf16)
     q_t = dot(p_orth, came[:, :span], ((0,), (0,))) / REPS
     q_out[...] = q_t
-    approx_out[...] = dot(p_orth.astype(f32), q_t, ((1,), (0,)), HIGHEST).astype(bf16)
+    q_high = q_t.astype(bf16)
+    q_low = (q_t - q_high.astype(f32)).astype(bf16)
+    approx = dot(p_orth, q_high, ((1,), (0,))) + dot(p_orth, q_low, ((1,), (0,)))
+    approx_out[...] = approx.astype(bf16)
 
 
 def middle(came, span):

time: 110 us -> 110 us (level)
  no operation moved by 1% of the time
where the time goes in v4:
time: 110 us
  starting transfers between devices  55.7 us (51%)
  waiting for transfers between devices  22.1 us (20%)
  blocking collectives  15 us (14%)
  Pallas kernels  6.78 us (6%)
  other arithmetic  5.33 us (5%)
  local copies, waits for them, and re-layouts  3.95 us (4%)
    ppermute x12, starting transfers between devices, swap(): lax.ppermute(x, axis, [(i, i ^ bits) for i in range(lax.axis_size(axis))])  25.4 us
    all_to_all x1, blocking collectives, body(): lax.all_to_all(approx_cols.reshape(32, rows, narrow), ROW, 0, 0, tiled=True)  15 us
    all_to_all x1, waiting for transfers between devices, body(): lax.all_to_all(jnp.concatenate([d_rows, p_rows], axis=2), ROW, 0, 0, tile...  11.9 us
    all_to_all x1, starting transfers between devices, body(): lax.all_to_all(jnp.concatenate([d_rows, p_rows], axis=2), ROW, 0, 0, tile...  11.3 us
    ppermute x4, starting transfers between devices, body(): lax.ppermute(q_t[quarter * s:quarter * (s + 1)], ('y', 'zl'), [(a * 4 + b...  9.73 us
    all_to_all x2, starting transfers between devices, along_y(): return lax.all_to_all(a, 'y', 0, 0, tiled=True)  9.28 us
    ppermute x4, waiting for transfers between devices, body(): lax.ppermute(q_t[quarter * s:quarter * (s + 1)], ('y', 'zl'), [(a * 4 + b...  4.76 us
    pallas_call x1, Pallas kernels, middle(): pl.pallas_call(mid_kernel, out_shape=(jax.ShapeDtypeStruct((64, span), f3...  4.27 us
  transfers between devices with their start and end apart: 19, of which 11 were waited for; matrix products, arithmetic and copies ran while one was open for 4% of the time, Pallas kernels for 1%

profile of v4, /device:TPU:1, one launch (start us, length us, event | category | flops | bytes accessed | tf_op | source)
XLA Modules:
  0.0 109.7 jit_solution(11290989187787638988)
XLA Ops:
  0.6 1.4 %copy-done = bf16[1,16,53248]{2,1,0:T(8,128)(2,1)S(1)} copy-done((bf16[1,16,53248]{2,1,0:T(8,128)(2,1)S(1)}, bf16[1,16,53248]{2,1,0:T(8,128)(2,1)}, u32[]{:S(2)}) %copy-start) | copy-done | bytes 1703960
  2.1 1.3 %split_kernel.1 = (bf16[4,16,6656]{2,1,0:T(8,128)(2,1)}, bf16[4,16,6656]{2,1,0:T(8,128)(2,1)}) custom-call(s32[1]{0:T(128)} %bitcast.1.zh, bf16[16,53248]{1,0:T(8,128)(2,1)S(1)} %bitcast.39), custom_call_target="tpu_custom_call" | custom-call | bytes 4194304 | tf_op jit(solution)/shard_map/split_kernel/pallas_call | solution.py:53
  3.4 5.0 %all-to-all-start = ((bf16[4,16,6656]{2,1,0:T(8,128)(2,1)}), bf16[4,16,6656]{2,1,0:T(8,128)(2,1)S(1)}, u32[]{:S(2)}, u32[]{:S(2)}) async-start(bf16[4,16,6656]{2,1,0:T(8,128)(2,1)} %get-tuple-element.21), calls=%async_computation | async-start | bytes 1703936 | tf_op jit(solution)/shard_map/delta_give/all_to_all | solution.py:160
  9.1 7.0 %collective-permute-start.3 = (bf16[16,1664]{1,0:T(8,128)(2,1)S(1)}, bf16[16,1664]{1,0:T(8,128)(2,1)S(1)}, u32[]{:S(2)}, u32[]{:S(2)}) collective-permute-start(bf16[16,1664]{1,0:T(8,128)(2,1)S(1)} %get-tuple-element.45), channel_id=1, source_target_pairs={{0,24},{8,88},{16,152},{24,216},{64,16},{72,80},{80,144},{88,208},... | collective-permute-start | bytes 159752 | tf_op jit(solution)/shard_map/q_z/ppermute | solution.py:169
  16.1 2.1 %collective-permute-start.2 = (bf16[16,1664]{1,0:T(8,128)(2,1)S(1)}, bf16[16,1664]{1,0:T(8,128)(2,1)S(1)}, u32[]{:S(2)}, u32[]{:S(2)}) collective-permute-start(bf16[16,1664]{1,0:T(8,128)(2,1)S(1)} %get-tuple-element.46), channel_id=1, source_target_pairs={{0,16},{8,80},{16,144},{24,208},{64,24},{72,88},{80,152},{88,216},... | collective-permute-start | bytes 159752 | tf_op jit(solution)/shard_map/q_z/ppermute | solution.py:169
  18.2 4.7 %collective-permute-done.3 = bf16[16,1664]{1,0:T(8,128)(2,1)S(1)} collective-permute-done((bf16[16,1664]{1,0:T(8,128)(2,1)S(1)}, bf16[16,1664]{1,0:T(8,128)(2,1)S(1)}, u32[]{:S(2)}, u32[]{:S(2)}) %collective-permute-start.3) | collective-permute-done | bytes 53280 | tf_op jit(solution)/shard_map/q_z/ppermute | solution.py:169
  23.0 3.6 %collective-permute-start.6 = (bf16[64,1664]{1,0:T(8,128)(2,1)S(1)}, bf16[64,1664]{1,0:T(8,128)(2,1)S(1)}, u32[]{:S(2)}, u32[]{:S(2)}) collective-permute-start(bf16[64,1664]{1,0:T(8,128)(2,1)S(1)} %pad_maximum_fusion.1.refs_0_), channel_id=1, source_target_pairs={{0,4},{2,6},{4,0},{6,2},{1,5},{3,7},{5,1},{7,3},{8,12},{10,14},{12... | collective-permute-start | bytes 638984 | tf_op jit(solution)/shard_map/q_x/ppermute | solution.py:25
  27.4 4.3 %all-to-all-start.1 = ((bf16[4,16,6656]{2,1,0:T(8,128)(2,1)}), bf16[4,16,6656]{2,1,0:T(8,128)(2,1)S(1)}, u32[]{:S(2)}, u32[]{:S(2)}) async-start(bf16[4,16,6656]{2,1,0:T(8,128)(2,1)} %get-tuple-element.24), calls=%async_computation.1 | async-start | bytes 1703936 | tf_op jit(solution)/shard_map/delta_keep/all_to_all | solution.py:160
  32.9 6.0 %collective-permute-start.15 = (bf16[2,16,6656]{2,1,0:T(8,128)(2,1)}, bf16[2,16,6656]{2,1,0:T(8,128)(2,1)}, u32[]{:S(2)}, u32[]{:S(2)}) collective-permute-start(bf16[2,16,6656]{2,1,0:T(8,128)(2,1)} %pad_maximum_fusion), channel_id=1, source_target_pairs={{0,32},{32,0},{1,33},{33,1},{2,34},{34,2},{3,35},{35,3},{4,36},{36... | collective-permute-start | bytes 1277960 | tf_op jit(solution)/shard_map/sums_zh/ppermute | solution.py:25
  39.0 1.4 %all-to-all-done.1.refs_9_ = bf16[4,16,6656]{2,1,0:T(8,128)(2,1)S(1)} async-done(((bf16[4,16,6656]{2,1,0:T(8,128)(2,1)}), bf16[4,16,6656]{2,1,0:T(8,128)(2,1)S(1)}, u32[]{:S(2)}, u32[]{:S(2)}) %all-to-all-start.1) | async-done | bytes 852000 | tf_op jit(solution)/shard_map/delta_keep/all_to_all | solution.py:160
  40.4 5.2 %collective-permute-start.7 = (bf16[64,1664]{1,0:T(8,128)(2,1)S(1)}, bf16[64,1664]{1,0:T(8,128)(2,1)S(1)}, u32[]{:S(2)}, u32[]{:S(2)}) collective-permute-start(bf16[64,1664]{1,0:T(8,128)(2,1)S(1)} %pad_maximum_fusion.1.refs_0_), channel_id=1, source_target_pairs={{0,1},{1,0},{2,3},{3,2},{4,5},{5,4},{6,7},{7,6},{8,9},{9,8},{10,11... | collective-permute-start | bytes 638984 | tf_op jit(solution)/shard_map/q_c/ppermute | solution.py:25
  47.7 1.2 %p_kernel.1 = f32[16,128]{1,0:T(8,128)S(1)} custom-call(s32[2,8]{1,0:T(2,128)S(1)} %pad_add_fusion.places, bf16[64,1664]{1,0:T(8,128)(2,1)S(1)} %pad_maximum_fusion.1.refs_0_, bf16[64,1664]{1,0:T(8,128)(2,1)S(1)} %collective-permute-done.4.refs_1_, bf16[64,1664]{1,0:T(8,128)(2,1)S(1)} %collective-permute-done.5.refs_2_, ...), custom_call_target="tpu_custom_call" | custom-call | flops 134217728 | bytes 3145728 | tf_op jit(solution)/shard_map/p_part/p_kernel/pallas_call | solution.py:80
  48.9 1.1 %collective-permute-start.13 = (f32[16,128]{1,0:T(8,128)S(1)}, f32[16,128]{1,0:T(8,128)S(1)}, u32[]{:S(2)}, u32[]{:S(2)}) collective-permute-start(f32[16,128]{1,0:T(8,128)S(1)} %p_kernel.1), channel_id=1, source_target_pairs={{0,128},{64,192},{128,0},{192,64},{1,129},{65,193},{129,1},{193,65... | collective-permute-start | bytes 24584 | tf_op jit(solution)/shard_map/p_y/ppermute | solution.py:25
  50.1 1.6 %collective-permute-start.12 = (f32[16,128]{1,0:T(8,128)S(1)}, f32[16,128]{1,0:T(8,128)S(1)}, u32[]{:S(2)}, u32[]{:S(2)}) collective-permute-start(f32[16,128]{1,0:T(8,128)S(1)} %p_kernel.1), channel_id=1, source_target_pairs={{0,192},{64,128},{128,64},{192,0},{1,193},{65,129},{129,65},{193,1... | collective-permute-start | bytes 24584 | tf_op jit(solution)/shard_map/p_y/ppermute | solution.py:25
  51.7 0.9 slice_bitcast_fusion.1
  53.0 1.1 collective-permute-done.12
  54.2 6.4 %collective-permute-start.14 = (f32[16,128]{1,0:T(8,128)S(1)}, f32[16,128]{1,0:T(8,128)S(1)}, u32[]{:S(2)}, u32[]{:S(2)}) collective-permute-start(f32[16,128]{1,0:T(8,128)S(1)} %add_add_fusion), channel_id=1, source_target_pairs={{0,32},{32,0},{1,33},{33,1},{2,34},{34,2},{3,35},{35,3},{4,36},{36... | collective-permute-start | bytes 24584 | tf_op jit(solution)/shard_map/p_zh/ppermute | solution.py:25
  60.9 1.1 %collective-permute-done.14 = f32[16,128]{1,0:T(8,128)S(1)} collective-permute-done((f32[16,128]{1,0:T(8,128)S(1)}, f32[16,128]{1,0:T(8,128)S(1)}, u32[]{:S(2)}, u32[]{:S(2)}) %collective-permute-start.14) | collective-permute-done | bytes 8224 | tf_op jit(solution)/shard_map/p_zh/ppermute | solution.py:25
  63.7 11.3 %all-to-all-start.2 = ((bf16[32,16,384]{2,1,0:T(8,128)(2,1)}), bf16[32,16,384]{2,1,0:T(8,128)(2,1)S(1)}, u32[]{:S(2)}, u32[]{:S(2)}) async-start(bf16[32,16,384]{2,1,0:T(8,128)(2,1)} %fusion.4), calls=%async_computation.2 | async-start | bytes 786432 | tf_op jit(solution)/shard_map/send/all_to_all | solution.py:216
  75.0 1.9 %sqrt_add_fusion = (f32[16,6656]{1,0:T(8,128)S(1)}, f32[16,6656]{1,0:T(8,128)}) fusion(f32[16,6656]{1,0:T(8,128)S(1)} %get-tuple-element.38, bf16[2,16,6656]{2,1,0:T(8,128)(2,1)} %collective-permute-done.15, f32[16,6656]{1,0:T(8,128)S(1)} %copy-done.2), kind=kLoop, calls=%fused_computation.12 | loop fusion | flops 745472 | bytes 1916928 | tf_op jit(solution)/shard_map/second/add | solution.py:220
  76.9 11.9 %all-to-all-done.2 = bf16[32,16,384]{2,1,0:T(8,128)(2,1)S(1)} async-done(((bf16[32,16,384]{2,1,0:T(8,128)(2,1)}), bf16[32,16,384]{2,1,0:T(8,128)(2,1)S(1)}, u32[]{:S(2)}, u32[]{:S(2)}) %all-to-all-start.2) | async-done | bytes 393248 | tf_op jit(solution)/shard_map/send/all_to_all | solution.py:216
  88.8 4.3 %mid_kernel.1 = (f32[64,208]{1,0:T(8,128)}, bf16[512,208]{1,0:T(8,128)(2,1)S(1)}) custom-call(bf16[512,384]{1,0:T(8,128)(2,1)S(1)} %bitcast.40), custom_call_target="tpu_custom_call" | custom-call | flops 8589934592 | bytes 1048576 | tf_op jit(solution)/shard_map/middle/mid_kernel/pallas_call | solution.py:133
  93.0 15.0 %all_to_all.20 = bf16[32,16,208]{2,1,0:T(8,128)(2,1)S(1)} all-to-all(bf16[32,16,208]{2,1,0:T(8,128)(2,1)S(1)} %bitcast.41), channel_id=1, replica_groups=mesh['y'=4,'zh'=2,'zl'=4,'x'=4,'c'=2] {'zl','x','c'}, dimensions={0} | all-to-all | bytes 425984 | tf_op jit(solution)/shard_map/approx/all_to_all | solution.py:226
  108.7 1.0 multiply_divide_fusion
  (52 shorter events, 7.9 us)
Async XLA Ops:
  0.6 1.5 %copy-start = (bf16[1,16,53248]{2,1,0:T(8,128)(2,1)S(1)}, bf16[1,16,53248]{2,1,0:T(8,128)(2,1)}, u32[]{:S(2)}) copy-start(bf16[1,16,53248]{2,1,0:T(8,128)(2,1)} %param.4) | copy-start | bytes 5111812
  2.1 6.3 %copy-start.3 = (bf16[1664,64]{0,1:T(8,128)(2,1)S(1)}, bf16[1664,64]{0,1:T(8,128)(2,1)}, u32[]{:S(2)}) copy-start(bf16[1664,64]{0,1:T(8,128)(2,1)} %param.5) | copy-start | bytes 638980
  3.4 19.6 %all-to-all-start = ((bf16[4,16,6656]{2,1,0:T(8,128)(2,1)}), bf16[4,16,6656]{2,1,0:T(8,128)(2,1)S(1)}, u32[]{:S(2)}, u32[]{:S(2)}) async-start(bf16[4,16,6656]{2,1,0:T(8,128)(2,1)} %get-tuple-element.21), calls=%async_computation | async-start | bytes 1703936 | tf_op jit(solution)/shard_map/delta_give/all_to_all | solution.py:160
  8.4 9.7 %collective-permute-start = (bf16[16,1664]{1,0:T(8,128)(2,1)S(1)}, bf16[16,1664]{1,0:T(8,128)(2,1)S(1)}, u32[]{:S(2)}, u32[]{:S(2)}) collective-permute-start(bf16[16,1664]{1,0:T(8,128)(2,1)S(1)} %get-tuple-element.44), channel_id=1, source_target_pairs={{0,0},{8,64},{16,128},{24,192},{64,8},{72,72},{80,136},{88,200},{1... | collective-permute-start | bytes 159752 | tf_op jit(solution)/shard_map/q_z/ppermute | solution.py:169
  9.1 13.8 %collective-permute-start.3 = (bf16[16,1664]{1,0:T(8,128)(2,1)S(1)}, bf16[16,1664]{1,0:T(8,128)(2,1)S(1)}, u32[]{:S(2)}, u32[]{:S(2)}) collective-permute-start(bf16[16,1664]{1,0:T(8,128)(2,1)S(1)} %get-tuple-element.45), channel_id=1, source_target_pairs={{0,24},{8,88},{16,152},{24,216},{64,16},{72,80},{80,144},{88,208},... | collective-permute-start | bytes 159752 | tf_op jit(solution)/shard_map/q_z/ppermute | solution.py:169
  16.1 6.8 %collective-permute-start.2 = (bf16[16,1664]{1,0:T(8,128)(2,1)S(1)}, bf16[16,1664]{1,0:T(8,128)(2,1)S(1)}, u32[]{:S(2)}, u32[]{:S(2)}) collective-permute-start(bf16[16,1664]{1,0:T(8,128)(2,1)S(1)} %get-tuple-element.46), channel_id=1, source_target_pairs={{0,16},{8,80},{16,144},{24,208},{64,24},{72,88},{80,152},{88,216},... | collective-permute-start | bytes 159752 | tf_op jit(solution)/shard_map/q_z/ppermute | solution.py:169
  18.2 4.8 %collective-permute-start.1 = (bf16[16,1664]{1,0:T(8,128)(2,1)S(1)}, bf16[16,1664]{1,0:T(8,128)(2,1)S(1)}, u32[]{:S(2)}, u32[]{:S(2)}) collective-permute-start(bf16[16,1664]{1,0:T(8,128)(2,1)S(1)} %get-tuple-element.47), channel_id=1, source_target_pairs={{0,8},{8,72},{16,136},{24,200},{64,0},{72,64},{80,128},{88,192},{1... | collective-permute-start | bytes 159752 | tf_op jit(solution)/shard_map/q_z/ppermute | solution.py:169
  23.0 16.0 %collective-permute-start.6 = (bf16[64,1664]{1,0:T(8,128)(2,1)S(1)}, bf16[64,1664]{1,0:T(8,128)(2,1)S(1)}, u32[]{:S(2)}, u32[]{:S(2)}) collective-permute-start(bf16[64,1664]{1,0:T(8,128)(2,1)S(1)} %pad_maximum_fusion.1.refs_0_), channel_id=1, source_target_pairs={{0,4},{2,6},{4,0},{6,2},{1,5},{3,7},{5,1},{7,3},{8,12},{10,14},{12... | collective-permute-start | bytes 638984 | tf_op jit(solution)/shard_map/q_x/ppermute | solution.py:25
  26.6 12.4 %collective-permute-start.5 = (bf16[64,1664]{1,0:T(8,128)(2,1)S(1)}, bf16[64,1664]{1,0:T(8,128)(2,1)S(1)}, u32[]{:S(2)}, u32[]{:S(2)}) collective-permute-start(bf16[64,1664]{1,0:T(8,128)(2,1)S(1)} %pad_maximum_fusion.1.refs_0_), channel_id=1, source_target_pairs={{0,6},{2,4},{4,2},{6,0},{1,7},{3,5},{5,3},{7,1},{8,14},{10,12},{12... | collective-permute-start | bytes 638984 | tf_op jit(solution)/shard_map/q_x/ppermute | solution.py:25
  27.4 11.6 %collective-permute-start.4 = (bf16[64,1664]{1,0:T(8,128)(2,1)S(1)}, bf16[64,1664]{1,0:T(8,128)(2,1)S(1)}, u32[]{:S(2)}, u32[]{:S(2)}) collective-permute-start(bf16[64,1664]{1,0:T(8,128)(2,1)S(1)} %pad_maximum_fusion.1.refs_0_), channel_id=1, source_target_pairs={{0,2},{2,0},{4,6},{6,4},{1,3},{3,1},{5,7},{7,5},{8,10},{10,8},{12,... | collective-permute-start | bytes 638984 | tf_op jit(solution)/shard_map/q_x/ppermute | solution.py:25
  27.4 13.0 %all-to-all-start.1 = ((bf16[4,16,6656]{2,1,0:T(8,128)(2,1)}), bf16[4,16,6656]{2,1,0:T(8,128)(2,1)S(1)}, u32[]{:S(2)}, u32[]{:S(2)}) async-start(bf16[4,16,6656]{2,1,0:T(8,128)(2,1)} %get-tuple-element.24), calls=%async_computation.1 | async-start | bytes 1703936 | tf_op jit(solution)/shard_map/delta_keep/all_to_all | solution.py:160
  32.9 18.9 %collective-permute-start.15 = (bf16[2,16,6656]{2,1,0:T(8,128)(2,1)}, bf16[2,16,6656]{2,1,0:T(8,128)(2,1)}, u32[]{:S(2)}, u32[]{:S(2)}) collective-permute-start(bf16[2,16,6656]{2,1,0:T(8,128)(2,1)} %pad_maximum_fusion), channel_id=1, source_target_pairs={{0,32},{32,0},{1,33},{33,1},{2,34},{34,2},{3,35},{35,3},{4,36},{36... | collective-permute-start | bytes 1277960 | tf_op jit(solution)/shard_map/sums_zh/ppermute | solution.py:25
  40.4 6.3 %collective-permute-start.7 = (bf16[64,1664]{1,0:T(8,128)(2,1)S(1)}, bf16[64,1664]{1,0:T(8,128)(2,1)S(1)}, u32[]{:S(2)}, u32[]{:S(2)}) collective-permute-start(bf16[64,1664]{1,0:T(8,128)(2,1)S(1)} %pad_maximum_fusion.1.refs_0_), channel_id=1, source_target_pairs={{0,1},{1,0},{2,3},{3,2},{4,5},{5,4},{6,7},{7,6},{8,9},{9,8},{10,11... | collective-permute-start | bytes 638984 | tf_op jit(solution)/shard_map/q_c/ppermute | solution.py:25
  45.6 1.5 %collective-permute-start.8 = (bf16[64,1664]{1,0:T(8,128)(2,1)S(1)}, bf16[64,1664]{1,0:T(8,128)(2,1)S(1)}, u32[]{:S(2)}, u32[]{:S(2)}) collective-permute-start(bf16[64,1664]{1,0:T(8,128)(2,1)S(1)} %collective-permute-done.4.refs_1_), channel_id=1, source_target_pairs={{0,1},{1,0},{2,3},{3,2},{4,5},{5,4},{6,7},{7,6},{8,9},{9,8},{10,11... | collective-permute-start | bytes 638984 | tf_op jit(solution)/shard_map/q_c/ppermute | solution.py:25
  45.6 1.8 %collective-permute-start.9 = (bf16[64,1664]{1,0:T(8,128)(2,1)S(1)}, bf16[64,1664]{1,0:T(8,128)(2,1)S(1)}, u32[]{:S(2)}, u32[]{:S(2)}) collective-permute-start(bf16[64,1664]{1,0:T(8,128)(2,1)S(1)} %collective-permute-done.5.refs_2_), channel_id=1, source_target_pairs={{0,1},{1,0},{2,3},{3,2},{4,5},{5,4},{6,7},{7,6},{8,9},{9,8},{10,11... | collective-permute-start | bytes 638984 | tf_op jit(solution)/shard_map/q_c/ppermute | solution.py:25
  46.1 1.6 %collective-permute-start.10 = (bf16[64,1664]{1,0:T(8,128)(2,1)S(1)}, bf16[64,1664]{1,0:T(8,128)(2,1)S(1)}, u32[]{:S(2)}, u32[]{:S(2)}) collective-permute-start(bf16[64,1664]{1,0:T(8,128)(2,1)S(1)} %collective-permute-done.6.refs_3_), channel_id=1, source_target_pairs={{0,1},{1,0},{2,3},{3,2},{4,5},{5,4},{6,7},{7,6},{8,9},{9,8},{10,11... | collective-permute-start | bytes 638984 | tf_op jit(solution)/shard_map/q_c/ppermute | solution.py:25
  48.9 4.1 %collective-permute-start.13 = (f32[16,128]{1,0:T(8,128)S(1)}, f32[16,128]{1,0:T(8,128)S(1)}, u32[]{:S(2)}, u32[]{:S(2)}) collective-permute-start(f32[16,128]{1,0:T(8,128)S(1)} %p_kernel.1), channel_id=1, source_target_pairs={{0,128},{64,192},{128,0},{192,64},{1,129},{65,193},{129,1},{193,65... | collective-permute-start | bytes 24584 | tf_op jit(solution)/shard_map/p_y/ppermute | solution.py:25
  50.1 4.0 %collective-permute-start.12 = (f32[16,128]{1,0:T(8,128)S(1)}, f32[16,128]{1,0:T(8,128)S(1)}, u32[]{:S(2)}, u32[]{:S(2)}) collective-permute-start(f32[16,128]{1,0:T(8,128)S(1)} %p_kernel.1), channel_id=1, source_target_pairs={{0,192},{64,128},{128,64},{192,0},{1,193},{65,129},{129,65},{193,1... | collective-permute-start | bytes 24584 | tf_op jit(solution)/shard_map/p_y/ppermute | solution.py:25
  51.7 2.5 %collective-permute-start.11 = (f32[16,128]{1,0:T(8,128)S(1)}, f32[16,128]{1,0:T(8,128)S(1)}, u32[]{:S(2)}, u32[]{:S(2)}) collective-permute-start(f32[16,128]{1,0:T(8,128)S(1)} %p_kernel.1), channel_id=1, source_target_pairs={{0,64},{64,0},{128,192},{192,128},{1,65},{65,1},{129,193},{193,129... | collective-permute-start | bytes 24584 | tf_op jit(solution)/shard_map/p_y/ppermute | solution.py:25
  54.2 7.8 %collective-permute-start.14 = (f32[16,128]{1,0:T(8,128)S(1)}, f32[16,128]{1,0:T(8,128)S(1)}, u32[]{:S(2)}, u32[]{:S(2)}) collective-permute-start(f32[16,128]{1,0:T(8,128)S(1)} %add_add_fusion), channel_id=1, source_target_pairs={{0,32},{32,0},{1,33},{33,1},{2,34},{34,2},{3,35},{35,3},{4,36},{36... | collective-permute-start | bytes 24584 | tf_op jit(solution)/shard_map/p_zh/ppermute | solution.py:25
  62.0 13.0 %copy-start.2 = (f32[16,6656]{1,0:T(8,128)S(1)}, f32[16,6656]{1,0:T(8,128)}, u32[]{:S(2)}) copy-start(f32[16,6656]{1,0:T(8,128)} %param.7) | copy-start | bytes 1277956
  63.7 25.1 %all-to-all-start.2 = ((bf16[32,16,384]{2,1,0:T(8,128)(2,1)}), bf16[32,16,384]{2,1,0:T(8,128)(2,1)S(1)}, u32[]{:S(2)}, u32[]{:S(2)}) async-start(bf16[32,16,384]{2,1,0:T(8,128)(2,1)} %fusion.4), calls=%async_computation.2 | async-start | bytes 786432 | tf_op jit(solution)/shard_map/send/all_to_all | solution.py:216
  93.0 15.7 %copy-start.1 = (f32[16,6656]{1,0:T(8,128)S(1)}, f32[16,6656]{1,0:T(8,128)}, u32[]{:S(2)}) copy-start(f32[16,6656]{1,0:T(8,128)} %param.6) | copy-start | bytes 1277956
